TPU v7x, 256 devices: a whole 4x4x8 slice. The times are simulated.
256 devices in a mesh: ctx: 32 (over x, z), tr: 2 (over core), tc: 4 (over y).
Axes of the slice: x: 4, y: 4, z: 8, core: 2. Of those that a mesh axis runs over, the one named last changes fastest.
Arguments:
- tokens: bfloat16 [8192, 4096], P('ctx'), may hold values from -6 to 6
- w_in: bfloat16 [4096, 10240], P(('ctx', 'tr'), 'tc'), may hold values from -0.09375 to 0.09375
- w_step: bfloat16 [4096, 128], P(('ctx', 'tr'), 'tc'), may hold values from -0.09375 to 0.09375
- conv_weight: float32 [4, 10240], P(None, 'tc'), may hold values from -3 to 3
- conv_bias: float32 [10240], P('tc'), may hold values from -3 to 3
- dt_bias: float32 [128], P('tc'), may hold values from -5 to -3
- decay_rate: float32 [128], P('tc'), may hold values from 0.0012207031 to 2
- turn_keep: float32 [128], P('tc'), may hold values from 0.6 to 0.85
- skip: float32 [128], P('tc'), may hold values from 0.5 to 2
- norm_gain: float32 [8192], P('tc'), may hold values from 0.5 to 1.5
- gate: bfloat16 [8192, 8192], P(('ctx', 'tr'), 'tc'), may hold values from -6 to 6
- segment_ids: int32 [8192], replicated, may hold values from 0 to 5, never falling along the last dimension, each value on 1 to 4096 neighbouring positions
- turn_start: int32 [8192], P(('ctx', 'tr')), may hold values 0 or 1
Outputs:
- normed: bfloat16 [8192, 8192], P(('ctx', 'tr'), 'tc')
All inputs are finite; a program needn't handle non-finite values. No bound on the sum of `turn_start` on one device may be relied on, other than what follows from the above.
Results may differ from a plain program's by a relative error of at most 0.006.
Values may be sent and summed in bfloat16 or wider, within the bound.
A program may use at most 192 MiB of HBM per device.

v0:
```python
import jax
import jax.numpy as jnp
from jax import lax
from jax.sharding import PartitionSpec as P

HEAD_GROUP = 16
HEAD_DIM = 64
STATE = 128
SPAN = 128
INNER = 8192


EPSILON = 1e-05


def shifted(block, axis, distance):
    devices = range(lax.axis_size(axis))
    route = [(i - distance, i) for i in devices if i - distance in devices]
    return lax.ppermute(block, axis, route)


def prefix(part, axis, combine, identity):
    place = lax.axis_index(axis)
    gathered = jax.tree.map(lambda a: lax.all_gather(a, axis), part)
    state = jax.tree.map(lambda a, e: jnp.zeros_like(a) + jnp.asarray(e, a.dtype), part, identity)

    def one(hop, state):
        return combine(
            state, jax.tree.map(lambda a: lax.dynamic_index_in_dim(a, hop, 0, False), gathered)
        )

    return lax.fori_loop(0, place, one, state)


def shards(
    tokens,
    w_in,
    w_step,
    conv_weight,
    conv_bias,
    dt_bias,
    decay_rate,
    turn_keep,
    skip,
    norm_gain,
    gate,
    segment_ids,
    turn_start,
):
    row_count = gate.shape[0]
    core_index = lax.axis_index("tr")
    core_count = lax.axis_size("tr")
    device_place = lax.axis_index("ctx") * core_count + core_index
    own_rows = lax.dynamic_slice_in_dim(tokens, core_index * row_count, row_count, 0)
    summed_in = jnp.dot(
        own_rows,
        lax.all_gather(w_in, ("ctx", "tr"), axis=0, tiled=True),
        preferred_element_type=jnp.float32,
    )
    dt_raw = jnp.dot(
        own_rows,
        lax.all_gather(w_step, ("ctx", "tr"), axis=0, tiled=True),
        preferred_element_type=jnp.float32,
    )
    xbc = summed_in.astype(jnp.bfloat16)
    tap_count = conv_weight.shape[0]
    rim_rows = shifted(xbc[row_count - (tap_count - 1) :], ("ctx", "tr"), 1)
    padded_ids = jnp.concatenate([jnp.full((tap_count - 1,), -1, jnp.int32), segment_ids])
    extended_ids = lax.dynamic_slice_in_dim(
        padded_ids, device_place * row_count, row_count + tap_count - 1, 0
    )
    seg_ids = extended_ids[tap_count - 1 :]
    extended = jnp.concatenate([rim_rows, xbc], axis=0)
    conv_sum = jnp.zeros(xbc.shape, jnp.float32) + conv_bias[None, :]
    for tap_index in range(tap_count):
        tap_mask = (extended_ids[tap_index : tap_index + row_count] == seg_ids).astype(jnp.float32)
        conv_sum = (
            conv_sum
            + conv_weight[tap_index][None, :]
            * extended[tap_index : tap_index + row_count].astype(jnp.float32)
            * tap_mask[:, None]
        )
    mixed_rows = jax.nn.silu(conv_sum).astype(jnp.bfloat16)
    span_count = row_count // SPAN
    per_group = HEAD_GROUP * HEAD_DIM + 2 * STATE
    groups_here = conv_bias.shape[0] // per_group
    heads_here = decay_rate.shape[0]
    grouped = mixed_rows.reshape(span_count, SPAN, groups_here, per_group)
    head_input = grouped[..., : HEAD_GROUP * HEAD_DIM].reshape(
        span_count, SPAN, heads_here, HEAD_DIM
    )
    b_matrix = grouped[..., HEAD_GROUP * HEAD_DIM : HEAD_GROUP * HEAD_DIM + STATE]
    c_matrix = grouped[..., HEAD_GROUP * HEAD_DIM + STATE :]
    step_size = jax.nn.softplus(dt_raw + dt_bias[None, :]).reshape(span_count, SPAN, heads_here)
    turn_flags = turn_start.astype(jnp.float32).reshape(span_count, SPAN, 1)
    log_decay = (
        -decay_rate[None, None, :] * step_size + turn_flags * jnp.log(turn_keep)[None, None, :]
    )
    cumulative = jnp.cumsum(log_decay, axis=1)
    span_ids = seg_ids.reshape(span_count, SPAN)
    prior_ids = extended_ids[tap_count - 2 : tap_count - 2 + row_count].reshape(span_count, SPAN)[
        :, 0
    ]
    last_ids = span_ids[:, SPAN - 1]
    positions = jnp.arange(SPAN)
    allowed = (span_ids[:, :, None] == span_ids[:, None, :]) & (
        positions[:, None] >= positions[None, :]
    )[None, :, :]
    cum_heads = jnp.transpose(cumulative, (0, 2, 1)).reshape(
        span_count, groups_here, HEAD_GROUP, SPAN
    )
    step_heads = jnp.transpose(step_size, (0, 2, 1)).reshape(
        span_count, groups_here, HEAD_GROUP, SPAN
    )
    log_gap = cum_heads[..., :, None] - cum_heads[..., None, :]
    scores = jnp.einsum("ktgn,ksgn->kgts", c_matrix, b_matrix, preferred_element_type=jnp.float32)
    weights = (
        scores[:, :, None]
        * jnp.exp(jnp.where(allowed[:, None, None], log_gap, -jnp.inf))
        * step_heads[..., None, :]
    ).astype(jnp.bfloat16)
    weights = weights.reshape(span_count, heads_here, SPAN, SPAN)
    output_diag = jnp.einsum(
        "khts,kshp->kthp", weights, head_input, preferred_element_type=jnp.float32
    )
    to_end = jnp.where(
        (span_ids == last_ids[:, None])[:, :, None],
        jnp.exp(cumulative[:, SPAN - 1 :, :] - cumulative),
        0.0,
    )
    scaled = (head_input.astype(jnp.float32) * (to_end * step_size)[..., None]).astype(jnp.bfloat16)
    scaled_groups = scaled.reshape(span_count, SPAN, groups_here, HEAD_GROUP, HEAD_DIM)
    span_state = jnp.einsum(
        "ksgjp,ksgn->kgjpn", scaled_groups, b_matrix, preferred_element_type=jnp.float32
    )
    span_state = span_state.reshape(span_count, heads_here, HEAD_DIM, STATE)
    span_decay = (
        jnp.exp(cumulative[:, SPAN - 1, :]) * (last_ids == prior_ids).astype(jnp.float32)[:, None]
    )
    device_decay = span_decay[0]
    device_state = span_state[0]

    def compose(earlier, later):
        return (earlier[0] * later[0], later[0][:, None, None] * earlier[1] + later[1])

    identity = (jnp.ones_like(device_decay), jnp.zeros_like(device_state))
    incoming_decay, incoming = prefix(
        (device_decay, device_state), ("ctx", "tr"), compose, identity
    )
    start_list = [incoming]
    start_states = jnp.stack(start_list)
    state_high = start_states.astype(jnp.bfloat16)
    state_low = (start_states - state_high.astype(jnp.float32)).astype(jnp.bfloat16)
    both_states = jnp.stack([state_high, state_low], axis=1).reshape(
        span_count, 2, groups_here, HEAD_GROUP, HEAD_DIM, STATE
    )
    from_start = jnp.where((span_ids == prior_ids[:, None])[:, :, None], jnp.exp(cumulative), 0.0)
    off_parts = jnp.einsum(
        "ktgn,kigjpn->ktgjp", c_matrix, both_states, preferred_element_type=jnp.float32
    )
    output_off = off_parts.reshape(span_count, SPAN, heads_here, HEAD_DIM) * from_start[..., None]
    output_sum = (
        output_diag + output_off + skip[None, None, :, None] * head_input.astype(jnp.float32)
    )
    output_sum = output_sum.reshape(row_count, heads_here * HEAD_DIM)
    gated_rows = output_sum * jax.nn.silu(gate.astype(jnp.float32))
    square_sum = lax.psum(jnp.sum(gated_rows * gated_rows, axis=1), "tc")
    mean_sq = square_sum / INNER
    return (gated_rows * lax.rsqrt(mean_sq + EPSILON)[:, None] * norm_gain[None, :]).astype(
        jnp.bfloat16
    )


def solution(mesh):
    in_specs = (
        P("ctx", None),
        P(("ctx", "tr"), "tc"),
        P(("ctx", "tr"), "tc"),
        P(None, "tc"),
        P("tc"),
        P("tc"),
        P("tc"),
        P("tc"),
        P("tc"),
        P("tc"),
        P(("ctx", "tr"), "tc"),
        P(),
        P(("ctx", "tr")),
    )
    out_specs = P(("ctx", "tr"), "tc")
    return jax.shard_map(shards, mesh=mesh, in_specs=in_specs, out_specs=out_specs, check_vma=False)
```

profile of v0, /device:TPU:230, one launch (start us, length us, event | category | flops | bytes accessed | tf_op | source)
XLA Modules:
  0.0 494.6 jit_solution(8466418066449405587)
XLA Ops:
  9.4 48.0 %all-gather.1 = bf16[64,64,32]{1,2,0:T(8,128)(2,1)S(1)} all-gather(bf16[1,64,32]{1,2,0:T(8,128)(2,1)} %bitcast.112), channel_id=1, replica_groups=mesh['ctx'=32,'tr'=2,'tc'=4] {'ctx','tr'}, dimensions={0}, use_global_device_ids=true | all-gather | bytes 266240 | tf_op jit(solution)/shard_map/all_gather | solution.py:62
  60.0 57.1 %all-gather.5.cloned.1.call-done = bf16[4096,2560]{1,0:T(8,128)(2,1)} async-done(((bf16[64,2560]{1,0:T(8,128)(2,1)}), bf16[4096,2560]{1,0:T(8,128)(2,1)}) %all-gather.5.cloned.1.call-update) | async-done | bytes 20971536 | tf_op jit(solution)/shard_map/all_gather | solution.py:57
  117.1 9.8 %convolution_convert_fusion = bf16[128,2560]{1,0:T(8,128)(2,1)S(1)} fusion(bf16[4096,2560]{1,0:T(8,128)(2,1)} %all-gather.5.cloned.1.call-done, bf16[256,4096]{1,0:T(8,128)(2,1)S(1)} %copy-done, s32[]{:T(128)S(6)} %select_n.39), kind=kOutput, calls=%fused_computation.2 | convolution fusion | flops 2684682240 | bytes 22675460 | tf_op jit(solution)/shard_map/dot_general | solution.py:55
  127.0 2.2 collective-permute-start
  129.3 2.8 collective-permute-done
  137.4 2.2 fusion.12
  139.7 39.1 %all-gather = f32[64,1,32]{2,1,0:T(1,128)S(1)} all-gather(f32[1,1,32]{2,1,0:T(1,128)S(1)} %get-tuple-element.67), channel_id=2, replica_groups=mesh['ctx'=32,'tr'=2,'tc'=4] {'ctx','tr'}, dimensions={0}, use_global_device_ids=true | all-gather | bytes 8320 | tf_op jit(solution)/shard_map/all_gather | solution.py:24
  179.9 1.5 fusion.1
  181.4 192.8 %all-gather.7.cloned.1.call-done = f32[64,32,64,128]{3,2,1,0:T(8,128)} async-done(((f32[1,32,64,128]{3,2,1,0:T(8,128)}), f32[64,32,64,128]{3,2,1,0:T(8,128)}) %all-gather.7.cloned.1.call-update) | async-done | bytes 67108880 | tf_op jit(solution)/shard_map/all_gather | solution.py:24
  374.4 92.7 %while.12 = (s32[]{:T(128)}, f32[32,64,128]{2,1,0:T(8,128)S(1)}, s32[]{:T(128)}, f32[64,32]{1,0:T(8,128)S(1)}, f32[64,32,64,128]{3,2,1,0:T(8,128)}, /*index=5*/s32[]{:T(128)}, s32[]{:T(128)}, s32[]{:T(128)}) while((s32[]{:T(128)}, f32[32,64,128]{2,1,0:T(8,128)S(1)}, s32[]{:T(128)}, f32[64,32]{1,0:T(8,128)S(1)}, f32[64,32,64,128]{3,2,1,0:T(8,128)}, ...), condition=%wide.region_2.3_spmd, body=%wide.region_1.2_spmd.sunk | while | flops 524293 | bytes 3146239 | solution.py:32
  374.4 1.4 bitcast_add_fusion.2
  375.9 1.4 bitcast_add_fusion.2
  377.4 1.4 bitcast_add_fusion.2
  378.9 1.4 bitcast_add_fusion.2
  380.4 1.4 bitcast_add_fusion.2
  381.9 1.4 bitcast_add_fusion.2
  383.4 1.4 bitcast_add_fusion.2
  384.9 1.4 bitcast_add_fusion.2
  386.4 1.4 bitcast_add_fusion.2
  387.9 1.4 bitcast_add_fusion.2
  389.4 1.4 bitcast_add_fusion.2
  390.9 1.4 bitcast_add_fusion.2
  392.4 1.4 bitcast_add_fusion.2
  393.8 1.4 bitcast_add_fusion.2
  395.3 1.4 bitcast_add_fusion.2
  396.8 1.4 bitcast_add_fusion.2
  398.3 1.4 bitcast_add_fusion.2
  399.8 1.4 bitcast_add_fusion.2
  401.3 1.4 bitcast_add_fusion.2
  402.8 1.4 bitcast_add_fusion.2
  404.3 1.4 bitcast_add_fusion.2
  405.8 1.4 bitcast_add_fusion.2
  407.3 1.4 bitcast_add_fusion.2
  408.8 1.4 bitcast_add_fusion.2
  410.3 1.4 bitcast_add_fusion.2
  411.8 1.4 bitcast_add_fusion.2
  413.3 1.4 bitcast_add_fusion.2
  414.8 1.4 bitcast_add_fusion.2
  416.3 1.4 bitcast_add_fusion.2
  417.8 1.4 bitcast_add_fusion.2
  419.3 1.4 bitcast_add_fusion.2
  420.8 1.4 bitcast_add_fusion.2
  422.3 1.4 bitcast_add_fusion.2
  423.8 1.4 bitcast_add_fusion.2
  425.3 1.4 bitcast_add_fusion.2
  426.8 1.4 bitcast_add_fusion.2
  428.2 1.4 bitcast_add_fusion.2
  429.7 1.4 bitcast_add_fusion.2
  431.2 1.4 bitcast_add_fusion.2
  432.7 1.4 bitcast_add_fusion.2
  434.2 1.4 bitcast_add_fusion.2
  435.7 1.4 bitcast_add_fusion.2
  437.2 1.4 bitcast_add_fusion.2
  438.7 1.4 bitcast_add_fusion.2
  440.2 1.4 bitcast_add_fusion.2
  441.7 1.4 bitcast_add_fusion.2
  443.2 1.4 bitcast_add_fusion.2
  456.7 1.4 bitcast_add_fusion.2
  459.7 1.4 bitcast_add_fusion.2
  470.2 1.8 fusion.3
  472.0 1.6 copy.65
  473.5 1.5 multiply_reduce_fusion
  475.1 10.5 %psum.7 = f32[128]{0:T(128)S(1)} all-reduce(f32[128]{0:T(128)S(1)} %multiply_reduce_fusion), channel_id=1, replica_groups=mesh['ctx'=32,'tr'=2,'tc'=4] {'tc'}, use_global_device_ids=true, to_apply=%region_5.6 | all-reduce | flops 128 | bytes 1024 | tf_op jit(solution)/shard_map/psum | solution.py:167
  485.5 2.2 multiply_convert_fusion.1
  (141 shorter events, 33.8 us)
Async XLA Ops:
  6.5 51.6 %copy-start = (bf16[256,4096]{1,0:T(8,128)(2,1)S(1)}, bf16[256,4096]{1,0:T(8,128)(2,1)}, u32[]{:S(2)}) copy-start(bf16[256,4096]{1,0:T(8,128)(2,1)} %param.15) | copy-start | bytes 6291460
  6.5 51.5 %copy-start.12 = (s32[128]{0:T(128)S(1)}, s32[128]{0:T(128)}, u32[]{:S(2)}) copy-start(s32[128]{0:T(128)} %param.27) | copy-start | bytes 1540
  6.5 51.6 %copy-start.13 = (f32[32]{0:T(128)S(1)}, f32[32]{0:T(128)}, u32[]{:S(2)}) copy-start(f32[32]{0:T(128)} %param.22) | copy-start | bytes 388
  6.5 51.6 %copy-start.14 = (f32[32]{0:T(128)S(1)}, f32[32]{0:T(128)}, u32[]{:S(2)}) copy-start(f32[32]{0:T(128)} %param.21) | copy-start | bytes 388
  6.5 51.6 %copy-start.10 = (f32[32]{0:T(128)S(1)}, f32[32]{0:T(128)}, u32[]{:S(2)}) copy-start(f32[32]{0:T(128)} %param.20) | copy-start | bytes 388
  6.5 110.5 %all-gather.5.cloned.1.call-start = ((), (), s32[]{:S(2)}) async-start(), calls=%async_computation | async-start | bytes 21299200 | tf_op jit(solution)/shard_map/all_gather | solution.py:57
  7.3 367.0 %all-gather.7.cloned.1.call-start = ((), (), s32[]{:S(2)}) async-start(), calls=%async_computation.1 | async-start | bytes 68157440 | tf_op jit(solution)/shard_map/all_gather | solution.py:24
  59.9 69.2 %copy-start.7 = (f32[4,2560]{1,0:T(4,128)S(1)}, f32[4,2560]{1,0:T(4,128)}, u32[]{:S(2)}) copy-start(f32[4,2560]{1,0:T(4,128)} %param.18) | copy-start | bytes 122884
  59.9 72.1 %copy-start.8 = (f32[2560]{0:T(1024)S(1)}, f32[2560]{0:T(1024)}, u32[]{:S(2)}) copy-start(f32[2560]{0:T(1024)} %param.19) | copy-start | bytes 30724
  127.0 5.1 %collective-permute-start = (bf16[3,2560]{1,0:T(4,128)(2,1)S(1)}, bf16[3,2560]{1,0:T(4,128)(2,1)S(1)}, u32[]{:S(2)}, u32[]{:S(2)}) collective-permute-start(bf16[3,2560]{1,0:T(4,128)(2,1)S(1)} %slice.75), channel_id=1, source_target_pairs={{0,4},{4,8},{8,12},{12,16},{16,20},{20,24},{24,28},{28,32},{32,36}... | collective-permute-start | bytes 46088 | tf_op jit(solution)/shard_map/ppermute | solution.py:19
  133.5 0.8 copy-start.6
  134.3 0.8 copy-start.3
  137.4 2.2 copy-start.1
  467.6 1.4 copy-start.5
  468.8 1.2 copy-start.2
  468.8 1.4 copy-start.4
  468.8 1.3 copy-start.11
  473.5 12.0 %copy-start.9 = (f32[2048]{0:T(1024)S(1)}, f32[2048]{0:T(1024)}, u32[]{:S(2)}) copy-start(f32[2048]{0:T(1024)} %param.24) | copy-start | bytes 24580
Sparse Core Ops, SparseCore 0:
  10.1 106.9 all-gather.4
  139.7 234.4 all-gather.6
where the time goes:
time: 498 us; the launch traced here: 495 us
  waiting for transfers between devices  253 us (51%)
  other arithmetic  97.8 us (20%)
  blocking collectives  97.5 us (20%)
  matrix products  16.6 us (3%)
  between operations  14.4 us (3%)
  local copies, waits for them, and re-layouts  10.1 us (2%)
    all_gather x1, waiting for transfers between devices, prefix(): gathered = jax.tree.map(lambda a: lax.all_gather(a, axis), part)  193 us
    add x62, other arithmetic, compose(): later[0][:, None, None] * earlier[1] + later[1]  89.7 us
    all_gather x1, waiting for transfers between devices, shards(): lax.all_gather(w_in, ('ctx', 'tr'), axis=0, tiled=True)  57.1 us
    all_gather x1, blocking collectives, shards(): lax.all_gather(w_step, ('ctx', 'tr'), axis=0, tiled=True)  48 us
    all_gather x1, blocking collectives, prefix(): gathered = jax.tree.map(lambda a: lax.all_gather(a, axis), part)  39.1 us
    psum x1, blocking collectives, shards(): square_sum = lax.psum(jnp.sum(gated_rows * gated_rows, axis=1), 'tc')  10.5 us
  transfers between devices with their start and end apart: 3, of which 3 were waited for; matrix products, arithmetic and copies ran while one was open for 1% of the time, Pallas kernels for 0%

commit v1 on v0

v1 whole, which is shorter than its diff:
```python
import jax
import jax.numpy as jnp
from jax import lax
from jax.experimental import pallas as pl
from jax.experimental.pallas import tpu as pltpu
from jax.sharding import PartitionSpec as P

HEAD_GROUP = 16
HEAD_DIM = 64
STATE = 128
SPAN = 128
INNER = 8192
EPSILON = 1e-05

NX, NZ = 4, 8
ROWS = 256
SLAB = 1024
GROUP = 1280
WIDE = 1024
COLS = 256
CHUNKS = 5
RIM = 16
MESH = pl.DeviceIdType.MESH
F32, BF16 = jnp.float32, jnp.bfloat16
EXACT = lax.Precision.HIGHEST


def place():
    ctx = lax.axis_index("ctx")
    return lax.div(ctx, NZ), lax.rem(ctx, NZ), lax.axis_index("tr"), lax.axis_index("tc")


def turn(a, n):
    return lax.rem(a + n, n)


def remote(src, dst, send, recv, device):
    return pltpu.make_async_remote_copy(
        src_ref=src, dst_ref=dst, send_sem=send, recv_sem=recv, device_id=device, device_id_type=MESH
    )


def meet(devices):
    barrier = pltpu.get_barrier_semaphore()
    for device in devices:
        pl.semaphore_signal(barrier, inc=1, device_id=device, device_id_type=MESH)
    pl.semaphore_wait(barrier, len(devices))


def project_kernel(
    tokens, first, w_in, flags, xbc, dt, flags_out,
    toks, tok_relay, wg0, wg, part, rel_out, rel_in, nb_out, nb_in, dt_out, dt_in,
    s_local, s_tok, s_sib_s, s_sib_r, s_ring_s, s_ring_r, s_tok_s, s_tok_r, s_fwd_s, s_fwd_r,
    s_rel_s, s_rel_r, s_nb_s, s_nb_r, s_dt_s, s_dt_r, s_rim_s, s_rim_r, s_flag_s, s_flag_r,
):
    x, z, c, _ = place()
    ctx = lax.axis_index("ctx")
    at = lambda xx, zz: {"ctx": xx * NZ + zz}
    x_right, x_left, x_far = at(turn(x + 1, NX), z), at(turn(x + 3, NX), z), at(turn(x + 2, NX), z)
    z_right, z_left = at(x, turn(z + 1, NZ)), at(x, turn(z + 7, NZ))
    sibling = {"tr": 1 - c}
    after, before = {"ctx": turn(ctx + 1, NX * NZ)}, {"ctx": turn(ctx + NX * NZ - 1, NX * NZ)}

    local = []

    def fetch(src, dst):
        copy = pltpu.make_async_copy(src, dst, s_local.at[len(local)])
        copy.start()
        local.append(copy)

    def columns(group, j):
        return pl.ds(pl.multiple_of(group * GROUP + (j - 1) * COLS, 128), COLS)

    def slab(index):
        return pl.ds(pl.multiple_of(index * SLAB, 128), SLAB)

    fetch(first.at[c], wg0.at[z, c])
    for j in range(1, CHUNKS):
        fetch(w_in.at[:, columns(c, j)], wg.at[j - 1, z, c])
    own_tokens = pltpu.make_async_copy(tokens.at[:, slab(x)], toks.at[0], s_tok.at[0])
    own_flags = pltpu.make_async_copy(flags, flags_out.at[c], s_tok.at[1])
    own_tokens.start()
    own_flags.start()

    meet([x_right, x_left, x_far, x_far, z_right, z_left, sibling, after, before])

    started = []

    def send(copy):
        copy.start()
        started.append(copy)
        return copy

    from_sibling = [send(remote(first.at[1 - c], wg0.at[z, c], s_sib_s.at[0], s_sib_r.at[0], sibling))]
    for j in range(1, CHUNKS):
        from_sibling.append(
            send(remote(w_in.at[:, columns(1 - c, j)], wg.at[j - 1, z, c], s_sib_s.at[j], s_sib_r.at[j], sibling))
        )
    half = pl.multiple_of(c * 128, 128)
    relay_hop = [
        send(remote(tokens.at[pl.ds(half, 64), slab(turn(x + 2, NX))], tok_relay.at[0], s_tok_s.at[0], s_tok_r.at[0], x_right)),
        send(remote(tokens.at[pl.ds(half + 64, 64), slab(turn(x + 2, NX))], tok_relay.at[1], s_tok_s.at[1], s_tok_r.at[1], x_left)),
    ]
    near_hop = [
        send(remote(tokens.at[pl.ds(half, 128), slab(turn(x + 1, NX))], toks.at[3, pl.ds(half, 128)], s_tok_s.at[2], s_tok_r.at[2], x_right)),
        send(remote(tokens.at[pl.ds(half, 128), slab(turn(x + 3, NX))], toks.at[1, pl.ds(half, 128)], s_tok_s.at[3], s_tok_r.at[3], x_left)),
    ]
    flag_hop = send(remote(flags, flags_out.at[c], s_flag_s, s_flag_r, sibling))

    ring = {}

    def block(j, slot, piece=None):
        ref = wg0 if j == 0 else wg.at[j - 1]
        return ref.at[slot] if piece is None else ref.at[slot, piece]

    def ring_hop(j, h):
        if h == 0:
            local[j].wait()
            from_sibling[j].wait_recv()
        for way, sign, device in ((0, -1, z_right), (1, 1, z_left)):
            if h > 0:
                ring[way, h - 1, j].wait_recv()
            slot = turn(z + sign * h + NZ, NZ)
            piece = None if h < 3 else way
            ring[way, h, j] = send(
                remote(block(j, slot, piece), block(j, slot, piece), s_ring_s.at[way, h, j], s_ring_r.at[way, h, j], device)
            )

    relays, nears, rims, steps = {}, {}, {}, []

    def multiply(j):
        for way in range(2):
            ring[way, 3, j].wait_recv()
        if j == 0:
            w = wg0[:, :, :64, :].reshape(SLAB, COLS)
        else:
            w = wg[j - 1].reshape(SLAB, COLS)
        far = jnp.dot(toks[2], w, preferred_element_type=F32)
        rel_out[j, 0] = far[:128].astype(BF16)
        rel_out[j, 1] = far[128:].astype(BF16)
        for way, device in ((0, x_right), (1, x_left)):
            relays[way, j] = send(
                remote(rel_out.at[j, way], rel_in.at[j, way], s_rel_s.at[way, j], s_rel_r.at[way, j], device)
            )
        part[j, 1] = jnp.dot(toks[1], w, preferred_element_type=F32)
        part[j, 2] = jnp.dot(toks[3], w, preferred_element_type=F32)
        part[j, 0] = jnp.dot(toks[0], w, preferred_element_type=F32)

    def step_sums():
        heads = jnp.concatenate(
            [wg0[k, 0, 64:80, :128] + wg0[k, 1, 64:80, :128] for k in range(NZ)], axis=1
        )
        for d in (2, 1, 3, 0):
            sums = lax.dot_general(heads, toks[d], (((1,), (1,)), ((), ())), preferred_element_type=F32)
            if d == 0:
                dt[...] = sums
            else:
                dt_out[d - 1] = sums
                device = (x_right, x_far, x_left)[d - 1]
                steps.append(send(remote(dt_out.at[d - 1], dt_in.at[d - 1], s_dt_s.at[d - 1], s_dt_r.at[d - 1], device)))

    def pass_on(j):
        relays[0, j].wait_recv()
        nb_out[j, 0, :128] = (part[j, 1, :128] + rel_in[j, 0].astype(F32)).astype(BF16)
        nb_out[j, 0, 128:] = part[j, 1, 128:].astype(BF16)
        nears[0, j] = send(remote(nb_out.at[j, 0], nb_in.at[j, 0], s_nb_s.at[0, j], s_nb_r.at[0, j], x_right))
        relays[1, j].wait_recv()
        nb_out[j, 1, :128] = part[j, 2, :128].astype(BF16)
        nb_out[j, 1, 128:] = (part[j, 2, 128:] + rel_in[j, 1].astype(F32)).astype(BF16)
        nears[1, j] = send(remote(nb_out.at[j, 1], nb_in.at[j, 1], s_nb_s.at[1, j], s_nb_r.at[1, j], x_left))

    def finish(j):
        nears[0, j].wait_recv()
        nears[1, j].wait_recv()
        cols = pl.ds(WIDE if j == 0 else (j - 1) * COLS, COLS)
        xbc[RIM:, cols] = (part[j, 0] + (nb_in[j, 0].astype(F32) + nb_in[j, 1].astype(F32))).astype(BF16)
        rims[j] = send(remote(xbc.at[pl.ds(ROWS, RIM), cols], xbc.at[pl.ds(0, RIM), cols], s_rim_s.at[j], s_rim_r.at[j], after))

    relayed, forwards = [], []

    def relay_tokens():
        for way, device in ((0, x_right), (1, x_left)):
            relay_hop[way].wait_recv()
            rows = pl.ds(half + 64 * way, 64)
            relayed.append(send(remote(tok_relay.at[way], toks.at[2, rows], s_tok_s.at[4 + way], s_tok_r.at[4 + way], device)))

    def share_tokens():
        near_hop[0].wait_recv()
        near_hop[1].wait_recv()
        relayed[0].wait_recv()
        relayed[1].wait_recv()
        for d in (3, 1, 2):
            forwards.append(
                send(remote(toks.at[d, pl.ds(half, 128)], toks.at[d, pl.ds(half, 128)], s_fwd_s.at[d - 1], s_fwd_r.at[d - 1], sibling))
            )
        own_tokens.wait()
        for copy in forwards:
            copy.wait_recv()

    for tick in range(CHUNKS + 6):
        for h in (3, 2, 1, 0):
            if 0 <= tick - h < CHUNKS:
                ring_hop(tick - h, h)
        if tick == 1:
            relay_tokens()
        if tick == 4:
            share_tokens()
        if 0 <= tick - 4 < CHUNKS:
            multiply(tick - 4)
        if 0 <= tick - 5 < CHUNKS:
            pass_on(tick - 5)
        if tick == 4:
            step_sums()
        if 0 <= tick - 6 < CHUNKS:
            finish(tick - 6)
    for copy in steps:
        copy.wait_recv()
    dt[...] += dt_in[0] + dt_in[1] + dt_in[2]
    own_flags.wait()
    flag_hop.wait_recv()
    for j in range(CHUNKS):
        rims[j].wait_recv()
    for copy in started:
        copy.wait_send()


def project(tokens, first, w_in, flags):
    sem = pltpu.SemaphoreType.DMA
    return pl.pallas_call(
        project_kernel,
        out_shape=(
            jax.ShapeDtypeStruct((RIM + ROWS, GROUP), BF16),
            jax.ShapeDtypeStruct((HEAD_GROUP, ROWS), F32),
            jax.ShapeDtypeStruct((2, 8, 128), F32),
        ),
        in_specs=[pl.BlockSpec(memory_space=pl.ANY)] * 3 + [pl.BlockSpec(memory_space=pltpu.VMEM)],
        out_specs=[pl.BlockSpec(memory_space=pltpu.VMEM)] * 3,
        scratch_shapes=[
            pltpu.VMEM((NX, ROWS, SLAB), BF16),
            pltpu.VMEM((2, 64, SLAB), BF16),
            pltpu.VMEM((NZ, 2, 80, COLS), BF16),
            pltpu.VMEM((CHUNKS - 1, NZ, 2, 64, COLS), BF16),
            pltpu.VMEM((CHUNKS, 3, ROWS, COLS), F32),
            pltpu.VMEM((CHUNKS, 2, 128, COLS), BF16),
            pltpu.VMEM((CHUNKS, 2, 128, COLS), BF16),
            pltpu.VMEM((CHUNKS, 2, ROWS, COLS), BF16),
            pltpu.VMEM((CHUNKS, 2, ROWS, COLS), BF16),
            pltpu.VMEM((3, HEAD_GROUP, ROWS), F32),
            pltpu.VMEM((3, HEAD_GROUP, ROWS), F32),
            sem((CHUNKS,)),
            sem((2,)),
            sem((CHUNKS,)),
            sem((CHUNKS,)),
            sem((2, 4, CHUNKS)),
            sem((2, 4, CHUNKS)),
            sem((6,)),
            sem((6,)),
            sem((3,)),
            sem((3,)),
            sem((2, CHUNKS)),
            sem((2, CHUNKS)),
            sem((2, CHUNKS)),
            sem((2, CHUNKS)),
            sem((3,)),
            sem((3,)),
            sem((CHUNKS,)),
            sem((CHUNKS,)),
            sem,
            sem,
        ],
        compiler_params=pltpu.CompilerParams(
            collective_id=0, has_side_effects=True, vmem_limit_bytes=40 * 2**20
        ),
    )(tokens, first, w_in, flags)


def scan_kernel(
    xbc, dt, flags, gate, tok_col, tok_row, head_par, conv_par, chan_par, out,
    xs, osum, states, state_bf, columns, st_in, d_out, d_in, pre, tot_out, tot_in, e_out, e_in,
    back_out, back_in, gates, gated, gated_sib, sq_out, sq_in,
    s_gate, s_local, s_st_s, s_st_r, s_d_s, s_d_r, s_t_s, s_t_r, s_e_s, s_e_r, s_b_s, s_b_r, s_q_s, s_q_r, s_g_s, s_g_r, s_gate_r,
):
    x, z, c, y = place()
    z_peer = [None] + [{"ctx": x * NZ + turn(z + k, NZ)} for k in range(1, NZ)]
    x_peer = [None] + [{"ctx": turn(x + k, NX) * NZ + z} for k in range(1, NX)]
    row_peer = [
        {"tr": turn(c + a, 2), "tc": turn(y + b, 4)} for a in range(2) for b in range(4) if (a, b) != (0, 0)
    ]
    sibling = {"tr": 1 - c}
    own_cols = pl.ds(pl.multiple_of(c * WIDE, 128), WIDE)
    sib_cols = pl.ds(pl.multiple_of((1 - c) * WIDE, 128), WIDE)

    gate_local = pltpu.make_async_copy(gate.at[:, own_cols], gates.at[c], s_local)
    gate_local.start()
    meet(z_peer[1:] + x_peer[1:] + row_peer)
    started = []

    def send(copy):
        copy.start()
        started.append(copy)
        return copy

    gate_swap = send(remote(gate.at[:, sib_cols], gates.at[c], s_gate, s_gate_r, sibling))

    mine = head_par[pl.ds(pl.multiple_of(c * HEAD_GROUP, 8), HEAD_GROUP), :]
    step = jax.nn.softplus(dt[...] + mine[:, 0:1])
    turns = jnp.concatenate([flags[0, 0:1, :], flags[1, 0:1, :]], axis=1)
    log_decay = -mine[:, 1:2] * step + turns * mine[:, 2:3]
    row_at = lax.broadcasted_iota(jnp.int32, (SPAN, SPAN), 0)
    lane_at = lax.broadcasted_iota(jnp.int32, (SPAN, SPAN), 1)
    upper = (row_at <= lane_at).astype(F32)
    low_lanes = lane_at < HEAD_DIM
    spread_row = lax.broadcasted_iota(jnp.int32, (SPAN, WIDE), 0)
    spread_lane = lax.broadcasted_iota(jnp.int32, (SPAN, WIDE), 1)
    spread = (lax.shift_right_logical(spread_lane, 6) == spread_row - 32).astype(F32)

    cums, decays = [], []
    for b in range(2):
        span = slice(b * SPAN, (b + 1) * SPAN)
        cum = jnp.dot(log_decay[:, span], upper, precision=EXACT, preferred_element_type=F32)
        to_end = jnp.exp(cum[:, SPAN - 1 :] - cum) * step[:, span] * tok_row[2:3, span]
        from_start = jnp.exp(cum) * tok_row[1:2, span]
        rows = jnp.concatenate([cum, to_end, from_start, jnp.zeros((80, SPAN), F32)], axis=0)
        columns[b] = rows.T
        cums.append(cum)
        decays.append(jnp.dot(columns[b, 120:128], spread, precision=EXACT, preferred_element_type=F32)[7:8])

    def expand(b, first):
        return jnp.where(low_lanes, columns[b, :, first : first + 1], columns[b, :, first + 1 : first + 2])

    def conv(channel):
        cols = pl.ds(channel, 128)
        par = pl.ds(pl.multiple_of(c * GROUP + channel, 128), 128)
        ext = xbc[:, cols].astype(F32)
        total = conv_par[4:5, par] + jnp.zeros((ROWS, 128), F32)
        for k in range(3):
            total = total + conv_par[k : k + 1, par] * ext[RIM - 3 + k : RIM - 3 + k + ROWS] * tok_col[:, k : k + 1]
        total = total + conv_par[3:4, par] * ext[RIM:]
        return jax.nn.silu(total).astype(BF16)

    b_matrix, c_matrix = conv(WIDE), conv(WIDE + STATE)
    b_turned = [b_matrix[b * SPAN : (b + 1) * SPAN].T for b in range(2)]

    for pair in range(8):
        cols = slice(pair * 128, (pair + 1) * 128)
        heads = conv(pair * 128)
        xs[:, cols] = heads
        for b in range(2):
            scaled = (heads[b * SPAN : (b + 1) * SPAN].astype(F32) * expand(b, 16 + 2 * pair)).astype(BF16)
            states[b, :, cols] = jnp.dot(b_turned[b], scaled, preferred_element_type=F32)
        state_bf[:, :, cols] = (
            (decays[1][:, cols] * states[0, :, cols] + states[1, :, cols]).astype(BF16).reshape(NZ, 16, 128)
        )
    d_out[...] = columns[0, 120:128] * columns[1, 120:128]
    st_in[z] = state_bf[z]
    d_in[z] = d_out[...]
    st_hops, d_hops = [], []
    for k in range(1, NZ):
        d_hops.append(send(remote(d_out, d_in.at[z], s_d_s.at[k], s_d_r.at[k], z_peer[k])))
        st_hops.append(
            send(remote(state_bf.at[turn(z + k, NZ)], st_in.at[z], s_st_s.at[k], s_st_r.at[k], z_peer[k]))
        )

    for b in range(2):
        span = slice(b * SPAN, (b + 1) * SPAN)
        scores = lax.dot_general(
            c_matrix[span], b_matrix[span], (((1,), (1,)), ((), ())), preferred_element_type=F32
        )
        allowed = (tok_col[span, 3:4] == tok_row[0:1, span]) & (row_at >= lane_at)
        for pair in range(8):
            cols = slice(pair * 128, (pair + 1) * 128)
            halves = []
            for h in (2 * pair, 2 * pair + 1):
                gap = jnp.where(allowed, columns[b, :, h : h + 1] - cums[b][h : h + 1], -jnp.inf)
                halves.append((scores * jnp.exp(gap) * step[h : h + 1, span]).astype(BF16))
            heads = xs[span, cols]
            zero = jnp.zeros_like(heads)
            both = jnp.concatenate([jnp.where(low_lanes, heads, zero), jnp.where(low_lanes, zero, heads)], axis=0)
            diag = jnp.dot(jnp.concatenate(halves, axis=1), both, preferred_element_type=F32)
            skip = chan_par[0:1, pl.ds(pl.multiple_of(c * WIDE + pair * 128, 128), 128)]
            osum[span, cols] = diag + skip * heads.astype(F32)

    for hop in d_hops + st_hops:
        hop.wait_recv()
    per_chip = jnp.concatenate([d_in[k, 7:8] for k in range(NZ)], axis=0)
    wide = jnp.dot(per_chip, spread, precision=EXACT, preferred_element_type=F32)
    running, passed, ahead = jnp.zeros((16, WIDE), F32), jnp.ones((1, WIDE), F32), []
    row_decay = per_chip[0:1]
    for k in range(NZ):
        pre[k] = running
        ahead.append(passed)
        running = wide[k : k + 1] * running + st_in[k].astype(F32)
        passed = passed * wide[k : k + 1]
        if k:
            row_decay = row_decay * per_chip[k : k + 1]
    tot_out[...] = running.astype(BF16)
    e_out[...] = jnp.broadcast_to(row_decay, (8, 128))
    tot_in[x] = tot_out[...]
    e_in[x] = e_out[...]
    t_hops = []
    for k in range(1, NX):
        t_hops.append(send(remote(e_out, e_in.at[x], s_e_s.at[k], s_e_r.at[k], x_peer[k])))
        t_hops.append(send(remote(tot_out, tot_in.at[x], s_t_s.at[k], s_t_r.at[k], x_peer[k])))
    for hop in t_hops:
        hop.wait_recv()
    row_wide = jnp.dot(
        jnp.concatenate([e_in[k] for k in range(NX)], axis=0), spread, precision=EXACT, preferred_element_type=F32
    )
    entering = jnp.zeros((16, WIDE), F32)
    for k in range(NX):
        entering = jnp.where(k < x, row_wide[8 * k : 8 * k + 1] * entering + tot_in[k].astype(F32), entering)
    for k in range(NZ):
        back_out[k] = (pre[k] + ahead[k] * entering).astype(BF16)
    back_in[z] = back_out[z]
    b_hops = [
        send(remote(back_out.at[turn(z + k, NZ)], back_in.at[z], s_b_s.at[k], s_b_r.at[k], z_peer[k]))
        for k in range(1, NZ)
    ]
    gate_local.wait()
    gate_swap.wait_recv()
    for hop in b_hops:
        hop.wait_recv()

    squares = [jnp.zeros((SPAN, SPAN), F32)] * 2
    for pair in range(8):
        cols = slice(pair * 128, (pair + 1) * 128)
        carried = back_in[:, :, cols].reshape(STATE, 128)
        later = (decays[0][:, cols] * carried.astype(F32) + states[0, :, cols]).astype(BF16)
        for b, state in ((0, carried), (1, later)):
            span = slice(b * SPAN, (b + 1) * SPAN)
            off = jnp.dot(c_matrix[span], state, preferred_element_type=F32) * expand(b, 32 + 2 * pair)
            rows = (osum[span, cols] + off) * jax.nn.silu(gates[b, :, cols].astype(F32))
            gated[b, :, cols] = rows
            squares[b] = squares[b] + rows * rows
    swap = send(remote(gated.at[1 - c], gated_sib, s_g_s, s_g_r, sibling))
    sums = [jnp.sum(s.T, axis=0, keepdims=True) for s in squares]
    sq_out[...] = jnp.concatenate(sums + [jnp.zeros((6, SPAN), F32)], axis=0)
    q_hops = [
        send(remote(sq_out, sq_in.at[k], s_q_s.at[k], s_q_r.at[k], device)) for k, device in enumerate(row_peer)
    ]
    for hop in q_hops:
        hop.wait_recv()
    total = sq_out[...]
    for k in range(7):
        total = total + sq_in[k]
    scale = lax.rsqrt(total / INNER + EPSILON)
    scale = jnp.where(c == 0, scale[0:1], scale[1:2])
    scale = jnp.broadcast_to(scale, (SPAN, SPAN)).T[:, 0:1]
    out[:, own_cols] = (gated[c] * scale * chan_par[1:2, own_cols]).astype(BF16)
    swap.wait_recv()
    out[:, sib_cols] = (gated_sib[...] * scale * chan_par[1:2, sib_cols]).astype(BF16)
    for copy in started:
        copy.wait_send()


def scan(*arrays):
    sem = pltpu.SemaphoreType.DMA
    vmem = pl.BlockSpec(memory_space=pltpu.VMEM)
    return pl.pallas_call(
        scan_kernel,
        out_shape=jax.ShapeDtypeStruct((SPAN, 2 * WIDE), BF16),
        in_specs=[vmem] * 3 + [pl.BlockSpec(memory_space=pl.ANY)] + [vmem] * 5,
        out_specs=vmem,
        scratch_shapes=[
            pltpu.VMEM((ROWS, WIDE), BF16),
            pltpu.VMEM((ROWS, WIDE), F32),
            pltpu.VMEM((2, STATE, WIDE), F32),
            pltpu.VMEM((NZ, 16, WIDE), BF16),
            pltpu.VMEM((2, SPAN, 128), F32),
            pltpu.VMEM((NZ, 16, WIDE), BF16),
            pltpu.VMEM((8, 128), F32),
            pltpu.VMEM((NZ, 8, 128), F32),
            pltpu.VMEM((NZ, 16, WIDE), F32),
            pltpu.VMEM((16, WIDE), BF16),
            pltpu.VMEM((NX, 16, WIDE), BF16),
            pltpu.VMEM((8, 128), F32),
            pltpu.VMEM((NX, 8, 128), F32),
            pltpu.VMEM((NZ, 16, WIDE), BF16),
            pltpu.VMEM((NZ, 16, WIDE), BF16),
            pltpu.VMEM((2, SPAN, WIDE), BF16),
            pltpu.VMEM((2, SPAN, WIDE), F32),
            pltpu.VMEM((SPAN, WIDE), F32),
            pltpu.VMEM((8, 128), F32),
            pltpu.VMEM((7, 8, 128), F32),
            sem,
            sem,
            sem((NZ,)),
            sem((NZ,)),
            sem((NZ,)),
            sem((NZ,)),
            sem((NX,)),
            sem((NX,)),
            sem((NX,)),
            sem((NX,)),
            sem((NZ,)),
            sem((NZ,)),
            sem((7,)),
            sem((7,)),
            sem,
            sem,
            sem,
        ],
        compiler_params=pltpu.CompilerParams(
            collective_id=1, has_side_effects=True, vmem_limit_bytes=40 * 2**20
        ),
    )(*arrays)


def shards(
    tokens, w_in, w_step, conv_weight, conv_bias, dt_bias, decay_rate, turn_keep, skip, norm_gain, gate,
    segment_ids, turn_start,
):
    ctx, core = lax.axis_index("ctx"), lax.axis_index("tr")
    turned = w_step.T.reshape(2, HEAD_GROUP, 64)
    turned = jnp.where(core == 0, jnp.pad(turned, ((0, 0), (0, 0), (0, 192))), jnp.pad(turned, ((0, 0), (0, 0), (64, 128))))
    edges = jnp.stack([w_in[:, WIDE:GROUP], w_in[:, GROUP + WIDE :]])
    first = jnp.concatenate([edges, turned], axis=1)
    flags = jnp.broadcast_to(turn_start.astype(F32)[None, :], (8, SPAN))

    ids = lax.dynamic_slice_in_dim(
        jnp.concatenate([jnp.full((3,), -1, jnp.int32), segment_ids]), ctx * ROWS, ROWS + 3, 0
    )
    own = ids[3:]
    blocks = own.reshape(2, SPAN)
    prior = jnp.stack([ids[2], own[SPAN - 1]])
    tok_col = jnp.stack([(ids[k : k + ROWS] == own).astype(F32) for k in range(3)] + [own.astype(F32)], axis=1)
    tok_col = jnp.pad(tok_col, ((0, 0), (0, 124)))
    tok_row = jnp.stack(
        [
            own.astype(F32),
            (blocks == prior[:, None]).astype(F32).reshape(-1),
            (blocks == blocks[:, SPAN - 1 :]).astype(F32).reshape(-1),
        ]
    )
    tok_row = jnp.pad(tok_row, ((0, 5), (0, 0)))
    head_par = jnp.pad(jnp.stack([dt_bias, decay_rate, jnp.log(turn_keep)], axis=1), ((0, 0), (0, 125)))
    conv_par = jnp.concatenate([conv_weight, conv_bias[None], jnp.zeros((3, 2 * GROUP), F32)], axis=0)
    chan_par = jnp.concatenate(
        [jnp.repeat(skip, HEAD_DIM)[None], norm_gain[None], jnp.zeros((6, 2 * WIDE), F32)], axis=0
    )
    xbc, dt, both_flags = project(tokens, first, w_in, flags)
    return scan(xbc, dt, both_flags, gate, tok_col, tok_row, head_par, conv_par, chan_par)


def solution(mesh):
    in_specs = (
        P("ctx", None),
        P(("ctx", "tr"), "tc"),
        P(("ctx", "tr"), "tc"),
        P(None, "tc"),
        P("tc"),
        P("tc"),
        P("tc"),
        P("tc"),
        P("tc"),
        P("tc"),
        P(("ctx", "tr"), "tc"),
        P(),
        P(("ctx", "tr")),
    )
    out_specs = P(("ctx", "tr"), "tc")
    return jax.shard_map(shards, mesh=mesh, in_specs=in_specs, out_specs=out_specs, check_vma=False)
```

time: 498 us -> 112 us (0.22)
  the two profiles are of different devices: /device:TPU:230 before, /device:TPU:1 now
where the time goes in v1:
time: 112 us; the launch traced here: 111 us
  Pallas kernels  97.7 us (87%)
  local copies, waits for them, and re-layouts  8.32 us (7%)
  other arithmetic  5.28 us (5%)
    pallas_call x1, Pallas kernels, project(): pl.pallas_call(project_kernel, out_shape=(jax.ShapeDtypeStruct((RIM + ROW...  62.7 us
    pallas_call x1, Pallas kernels, scan(): pl.pallas_call(scan_kernel, out_shape=jax.ShapeDtypeStruct((SPAN, 2 * WID...  34.9 us
    unnamed x7, local copies, waits for them, and re-layouts  3.36 us

profile of v1, /device:TPU:1, one launch (start us, length us, event | category | flops | bytes accessed | tf_op | source)
XLA Modules:
  0.0 111.3 jit_solution(1079403342181872074)
XLA Ops:
  0.0 0.0 copy-start.1
  0.0 0.7 log_bitcast_fusion
  0.7 0.7 convert_element_type.34
  1.4 0.1 pad.31.clone
  1.5 0.1 pad.28.clone
  1.5 0.8 pad_dynamic-slice_fusion
  2.3 0.6 fusion
  2.9 1.3 %pad_add_fusion = s32[2]{0:T(128)S(1)} fusion(s32[1]{0:T(128)} %get-tuple-element.19, s32[1]{0:T(128)} %get-tuple-element.18), kind=kLoop, calls=%fused_computation.18 | loop fusion | flops 2 | bytes 16 | tf_op jit(solution)/shard_map/stack | solution.py:525
  4.2 0.7 pad_maximum_fusion.2
  4.9 0.1 slice_bitcast_fusion.2
  4.9 0.2 slice_reduce_fusion
  5.1 0.1 compare_convert_fusion.1
  5.2 0.7 broadcast_in_dim.23
  5.9 0.1 copy.32
  6.0 0.8 pad_select_fusion
  6.9 0.7 broadcast_in_dim.25
  7.6 0.1 broadcast_in_dim_reshape.3
  7.7 0.8 maximum_maximum_fusion.1.chan_par
  8.5 0.8 slice_bitcast_fusion.1
  9.3 0.9 maximum_maximum_fusion.conv_par
  10.1 0.1 copy.31
  10.3 0.0 copy-start
  10.3 1.6 %copy-done = bf16[256,4096]{1,0:T(8,128)(2,1)S(1)} copy-done((bf16[256,4096]{1,0:T(8,128)(2,1)S(1)}, bf16[256,4096]{1,0:T(8,128)(2,1)}, u32[]{:S(2)}) %copy-start) | copy-done | bytes 2097176
  11.9 0.0 copy-start.2
  11.9 1.0 copy-done.2
  12.8 62.7 %shard_map.127 = (bf16[272,1280]{1,0:T(8,128)(2,1)S(1)}, f32[16,256]{1,0:T(8,128)S(1)}, f32[2,8,128]{2,1,0:T(8,128)S(1)}) custom-call(bf16[256,4096]{1,0:T(8,128)(2,1)S(1)} %copy-done, bf16[2,80,256]{2,1,0:T(8,128)(2,1)S(1)} %pad_maximum_fusion.first, bf16[64,2560]{1,0:T(8,128)(2,1)S(1)} %copy-done.2, f32[8,128]{1,0:T(8,128)S(1)} %broadcast_in_dim.22.flags), custom_call_target="tpu_custom_call" | custom-call | tf_op jit(solution)/shard_map/pallas_call | solution.py:229
  75.6 0.0 copy-done.1
  75.6 34.9 %shard_map.128 = bf16[128,2048]{1,0:T(8,128)(2,1)S(1)} custom-call(bf16[272,1280]{1,0:T(8,128)(2,1)S(1)} %get-tuple-element.8.xbc, f32[16,256]{1,0:T(8,128)S(1)} %get-tuple-element.9.dt, f32[2,8,128]{2,1,0:T(8,128)S(1)} %get-tuple-element.10.flags, bf16[128,2048]{1,0:T(8,128)(2,1)S(1)} %copy-done.1, f32[256,128]{1,0:T(8,128)S(1)} %pad.23.tok_col, ...), custom_call_target="tpu_custom_call" | custom-call | tf_op jit(solution)/shard_map/pallas_call | solution.py:459
  110.5 0.8 copy.34
  (8 shorter events, 0.1 us)
Async XLA Ops:
  0.0 75.6 %copy-start.1 = (bf16[128,2048]{1,0:T(8,128)(2,1)S(1)}, bf16[128,2048]{1,0:T(8,128)(2,1)}, u32[]{:S(2)}) copy-start(bf16[128,2048]{1,0:T(8,128)(2,1)} %gate.1) | copy-start | bytes 1572868
  10.3 1.6 %copy-start = (bf16[256,4096]{1,0:T(8,128)(2,1)S(1)}, bf16[256,4096]{1,0:T(8,128)(2,1)}, u32[]{:S(2)}) copy-start(bf16[256,4096]{1,0:T(8,128)(2,1)} %tokens.1) | copy-start | bytes 6291460
  11.9 1.0 copy-start.2

commit v2 on v0

v2 whole, which is shorter than its diff:
```python
import jax
import jax.numpy as jnp
from jax import lax
from jax.experimental import pallas as pl
from jax.experimental.pallas import tpu as pltpu
from jax.sharding import PartitionSpec as P

HEAD_GROUP = 16
HEAD_DIM = 64
STATE = 128
SPAN = 128
INNER = 8192
EPSILON = 1e-05

NX, NZ = 4, 8
ROWS = 256
SLAB = 1024
GROUP = 1280
WIDE = 1024
COLS = 256
CHUNKS = 5
RIM = 16
MESH = pl.DeviceIdType.MESH
F32, BF16 = jnp.float32, jnp.bfloat16
EXACT = lax.Precision.HIGHEST


def place():
    ctx = lax.axis_index("ctx")
    return lax.div(ctx, NZ), lax.rem(ctx, NZ), lax.axis_index("tr"), lax.axis_index("tc")


def turn(a, n):
    return lax.rem(a + n, n)


def remote(src, dst, send, recv, device):
    return pltpu.make_async_remote_copy(
        src_ref=src, dst_ref=dst, send_sem=send, recv_sem=recv, device_id=device, device_id_type=MESH
    )


def meet(devices):
    barrier = pltpu.get_barrier_semaphore()
    for device in devices:
        pl.semaphore_signal(barrier, inc=1, device_id=device, device_id_type=MESH)
    pl.semaphore_wait(barrier, len(devices))


ORDER = (
    "r02", "r01", "r00", "relay", "r12", "r11", "r10", "r22", "r20", "near", "r32", "r03", "far", "r30",
    "r21", "toks", "mul2", "r04", "mul0", "r31", "pass2", "r13", "r14", "mul1", "flags", "pass0", "r23",
    "r24", "pass1", "r33", "steps", "r34", "fin0", "fin2", "mul3", "mul4", "dt", "bc", "pass3", "fin1", "st2",
    "pass4", "fin3", "st1", "diag2", "diag1", "st3", "zs2", "fin4", "zs1", "st4", "xs2", "xs1", "zs3", "zs4",
    "xs3", "diag3", "xs4", "diag4", "out1", "out3", "out2", "out4",
)


def layer_kernel(
    tokens, w_in, w_step_hbm, conv_w_hbm, conv_b_hbm, dt_bias_hbm, rate_hbm, keep_hbm, skip_hbm, gain_hbm, gate, ids_hbm,
    turns_hbm, out, w_step, conv_w, conv_b, dt_bias, rate, keep, skip_row, par, gain, ids, turns,
    toks, tok_relay, wg0, wg, step_rows, part, rel_out, rel_in, nb_out, nb_in, dt_out, dt_in, dt_own, flags,
    xbc, id_col, masks, spread, head_col, columns, wide_row, bc, xs, osum, states, state_bf, st_in, d_out, d_in,
    wide_z, pre, tot_out, tot_in, e_out, e_in, wide_x, back_out, back_in, gates, gated, gated_sib, squares, sq_out, sq_in,
    s_small, s_local, s_own, s_sib_s, s_sib_r, s_ring_s, s_ring_r, s_tok_s, s_tok_r, s_fwd_s, s_fwd_r, s_rel_s, s_rel_r,
    s_nb_s, s_nb_r, s_dt_s, s_dt_r, s_rim_s, s_rim_r, s_flag_s, s_flag_r, s_gate_s, s_gate_r,
    s_st_s, s_st_r, s_d_s, s_d_r, s_t_s, s_t_r, s_e_s, s_e_r, s_b_s, s_b_r, s_q_s, s_q_r, s_g_s, s_g_r,
):
    x, z, c, y = place()
    ctx = lax.axis_index("ctx")
    at = lambda xx, zz: {"ctx": xx * NZ + zz}
    z_peer = [None] + [at(x, turn(z + k, NZ)) for k in range(1, NZ)]
    x_peer = [None] + [at(turn(x + k, NX), z) for k in range(1, NX)]
    row_peer = [
        {"tr": turn(c + a, 2), "tc": turn(y + b, 4)} for a in range(2) for b in range(4) if (a, b) != (0, 0)
    ]
    x_right, x_far, x_left = x_peer[1:]
    z_right, z_left = z_peer[1], z_peer[7]
    sibling = {"tr": 1 - c}
    after, before = {"ctx": turn(ctx + 1, NX * NZ)}, {"ctx": turn(ctx + NX * NZ - 1, NX * NZ)}

    def columns_of(group, j):
        start = WIDE if j == 0 else (j - 1) * COLS
        return pl.ds(pl.multiple_of(group * GROUP + start, 128), COLS)

    def slab(index):
        return pl.ds(pl.multiple_of(index * SLAB, 128), SLAB)

    def block(j, slot, piece=None):
        ref = wg0 if j == 0 else wg.at[j - 1]
        return ref.at[slot] if piece is None else ref.at[slot, piece]

    own_cols = pl.ds(pl.multiple_of(c * WIDE, 128), WIDE)
    sib_cols = pl.ds(pl.multiple_of((1 - c) * WIDE, 128), WIDE)

    small = []
    for k, (src, dst) in enumerate(
        (
            (w_step_hbm, w_step), (turns_hbm, turns), (ids_hbm, ids), (conv_w_hbm, conv_w), (conv_b_hbm, conv_b),
            (dt_bias_hbm, dt_bias), (rate_hbm, rate), (keep_hbm, keep), (skip_hbm, skip_row), (gain_hbm, gain),
        )
    ):
        small.append(pltpu.make_async_copy(src, dst, s_small.at[k]))
        small[-1].start()
    local = []
    for j in range(CHUNKS):
        target = wg0.at[z, c, pl.ds(0, 64)] if j == 0 else wg.at[j - 1, z, c]
        copy = pltpu.make_async_copy(w_in.at[:, columns_of(c, j)], target, s_local.at[j])
        copy.start()
        local.append(copy)
    own_tokens = pltpu.make_async_copy(tokens.at[:, slab(x)], toks.at[0], s_own.at[0])
    own_tokens.start()
    own_gate = pltpu.make_async_copy(gate.at[:, own_cols], gates.at[c], s_own.at[1])
    own_gate.start()

    small[0].wait()
    small[1].wait()
    weights = w_step[...].astype(F32)
    blank = jnp.zeros((2 * HEAD_GROUP, 64), F32)
    weights = jnp.where(
        c == 0, jnp.concatenate([weights, blank], axis=1), jnp.concatenate([blank, weights], axis=1)
    )
    for group in range(2):
        rows = weights[group * HEAD_GROUP : (group + 1) * HEAD_GROUP].astype(BF16)
        step_rows[group] = jnp.concatenate([rows, jnp.zeros((HEAD_GROUP, 128), BF16)], axis=1)
    wg0[z, c, 64:80, :] = step_rows[c]
    flags[c] = jnp.broadcast_to(turns[...].astype(F32), (8, SPAN))

    meet(z_peer[1:] + x_peer[1:] + row_peer + [after, before])

    started = []

    def send(src, dst, sems, index, device):
        if index is None:
            copy = remote(src, dst, sems[0], sems[1], device)
        else:
            copy = remote(src, dst, sems[0].at[index], sems[1].at[index], device)
        copy.start()
        started.append(copy)
        return copy

    sib = (s_sib_s, s_sib_r)
    from_sibling = [
        [
            send(w_in.at[:, columns_of(1 - c, 0)], wg0.at[z, c, pl.ds(0, 64)], sib, 0, sibling),
            send(step_rows.at[1 - c], wg0.at[z, c, pl.ds(64, 16)], sib, 5, sibling),
        ]
    ]
    for j in (2, 1, 3, 4):
        from_sibling.append([send(w_in.at[:, columns_of(1 - c, j)], wg.at[j - 1, z, c], sib, j, sibling)])
    from_sibling = [from_sibling[0], from_sibling[2], from_sibling[1], from_sibling[3], from_sibling[4]]
    half = pl.multiple_of(c * 128, 128)
    tok = (s_tok_s, s_tok_r)
    far_slab, right_slab, left_slab = (slab(turn(x + k, NX)) for k in (2, 1, 3))
    relay_hop = [
        send(tokens.at[pl.ds(half + 64 * way, 64), far_slab], tok_relay.at[way], tok, way, device)
        for way, device in ((0, x_right), (1, x_left))
    ]
    near_hop = [
        send(tokens.at[pl.ds(half, 128), right_slab], toks.at[3, pl.ds(half, 128)], tok, 2, x_right),
        send(tokens.at[pl.ds(half, 128), left_slab], toks.at[1, pl.ds(half, 128)], tok, 3, x_left),
    ]
    hops = {}

    def ring_hop(h, j):
        if h == 0:
            local[j].wait()
            for copy in from_sibling[j]:
                copy.wait_recv()
        for way, sign, device in ((0, -1, z_right), (1, 1, z_left)):
            if h > 0:
                hops["r", way, h - 1, j].wait_recv()
            slot = turn(z + sign * h + NZ, NZ)
            piece = None if h < 3 else way
            ref = block(j, slot, piece)
            hops["r", way, h, j] = send(ref, ref, (s_ring_s, s_ring_r), (way, h, j), device)

    row_at = lax.broadcasted_iota(jnp.int32, (SPAN, SPAN), 0)
    lane_at = lax.broadcasted_iota(jnp.int32, (SPAN, SPAN), 1)
    low_lanes = lane_at < HEAD_DIM
    id_rows = []

    def do_flags(_):
        hops["flag"] = send(flags.at[c], flags.at[c], (s_flag_s, s_flag_r), None, sibling)
        hops["gate"] = send(gate.at[:, sib_cols], gates.at[c], (s_gate_s, s_gate_r), None, sibling)
        for copy in small[2:]:
            copy.wait()
        prior = ids[pl.ds(jnp.maximum(2 * ctx - 1, 0), 1), :].astype(F32)
        id_rows.append(jnp.where(ctx == 0, -1.0, prior))
        for b in range(2):
            id_rows.append(ids[pl.ds(2 * ctx + b, 1), :].astype(F32))
        for b in range(3):
            id_col[b * SPAN : (b + 1) * SPAN] = jnp.broadcast_to(id_rows[b], (SPAN, SPAN)).T
        for k in range(3):
            masks[k] = (id_col[SPAN - 3 + k : SPAN - 3 + k + ROWS] == id_col[SPAN:]).astype(F32)
        rows = [jnp.concatenate([v[...], jnp.zeros((1, 96), F32)], axis=1) for v in (dt_bias, rate, keep, skip_row)]
        par[...] = jnp.concatenate(rows + [jnp.zeros((4, 128), F32)], axis=0)
        spread_row = lax.broadcasted_iota(jnp.int32, (SPAN, WIDE), 0)
        spread_lane = lax.shift_right_logical(lax.broadcasted_iota(jnp.int32, (SPAN, WIDE), 1), 6)
        spread[...] = (spread_lane == spread_row - 32).astype(F32)
        pick = (spread_lane == spread_row - c * HEAD_GROUP).astype(F32)
        wide_row[2] = jnp.dot(par[...], pick, precision=EXACT, preferred_element_type=F32)
        head_col[...] = jnp.concatenate([par[...], jnp.zeros((120, 128), F32)], axis=0).T

    def do_relay(_):
        for way, device in ((0, x_right), (1, x_left)):
            relay_hop[way].wait_recv()
            rows = pl.ds(half + 64 * way, 64)
            hops["relay", way] = send(tok_relay.at[way], toks.at[2, rows], tok, 4 + way, device)

    def share(d, way=None):
        rows = pl.ds(half, 128) if way is None else pl.ds(half + 64 * way, 64)
        ref, index = toks.at[d, rows], d - 1 if way is None else 3 * way + 1
        hops["share", index] = send(ref, ref, (s_fwd_s, s_fwd_r), index, sibling)

    def do_near(_):
        near_hop[0].wait_recv()
        share(3)
        near_hop[1].wait_recv()
        share(1)

    def do_far(_):
        for way in range(2):
            hops["relay", way].wait_recv()
            share(2, way)

    def do_toks(_):
        own_tokens.wait()
        for index in (0, 1, 2, 4):
            hops["share", index].wait_recv()

    def do_mul(j):
        for way in range(2):
            hops["r", way, 3, j].wait_recv()
        w = (wg0[:, :, :64, :] if j == 0 else wg[j - 1]).reshape(SLAB, COLS)
        far = jnp.dot(toks[2], w, preferred_element_type=F32)
        rel_out[j, 0] = far[:128].astype(BF16)
        rel_out[j, 1] = far[128:].astype(BF16)
        for way, device in ((0, x_right), (1, x_left)):
            hops["rel", way, j] = send(rel_out.at[j, way], rel_in.at[j, way], (s_rel_s, s_rel_r), (way, j), device)
        part[j, 1] = jnp.dot(toks[1], w, preferred_element_type=F32)
        part[j, 2] = jnp.dot(toks[3], w, preferred_element_type=F32)
        part[j, 0] = jnp.dot(toks[0], w, preferred_element_type=F32)

    def do_steps(_):
        heads = jnp.concatenate(
            [wg0[k, 0, 64:80, :128] + wg0[k, 1, 64:80, :128] for k in range(NZ)], axis=1
        )
        for d in (2, 1, 3, 0):
            sums = lax.dot_general(heads, toks[d], (((1,), (1,)), ((), ())), preferred_element_type=F32)
            if d == 0:
                dt_own[...] = sums
            else:
                dt_out[d - 1] = sums
                hops["dt", d] = send(dt_out.at[d - 1], dt_in.at[d - 1], (s_dt_s, s_dt_r), d - 1, x_peer[d])

    def do_pass(j):
        hops["rel", 0, j].wait_recv()
        nb_out[j, 0, :128] = (part[j, 1, :128] + rel_in[j, 0].astype(F32)).astype(BF16)
        nb_out[j, 0, 128:] = part[j, 1, 128:].astype(BF16)
        hops["nb", 0, j] = send(nb_out.at[j, 0], nb_in.at[j, 0], (s_nb_s, s_nb_r), (0, j), x_right)
        hops["rel", 1, j].wait_recv()
        nb_out[j, 1, :128] = part[j, 2, :128].astype(BF16)
        nb_out[j, 1, 128:] = (part[j, 2, 128:] + rel_in[j, 1].astype(F32)).astype(BF16)
        hops["nb", 1, j] = send(nb_out.at[j, 1], nb_in.at[j, 1], (s_nb_s, s_nb_r), (1, j), x_left)

    def do_fin(j):
        hops["nb", 0, j].wait_recv()
        hops["nb", 1, j].wait_recv()
        xbc[j, RIM:] = (part[j, 0] + (nb_in[j, 0].astype(F32) + nb_in[j, 1].astype(F32))).astype(BF16)
        hops["rim", j] = send(
            xbc.at[j, pl.ds(ROWS, RIM)], xbc.at[j, pl.ds(0, RIM)], (s_rim_s, s_rim_r), j, after
        )

    cums, steps, entered, left = [], [], [], []

    def do_dt(_):
        for d in (1, 2, 3):
            hops["dt", d].wait_recv()
        hops["flag"].wait_recv()
        mine = head_col[pl.ds(pl.multiple_of(c * HEAD_GROUP, 8), HEAD_GROUP), :]
        step = jax.nn.softplus(dt_own[...] + dt_in[0] + dt_in[1] + dt_in[2] + mine[:, 0:1])
        turned = jnp.concatenate([flags[0, 0:1, :], flags[1, 0:1, :]], axis=1)
        log_decay = -mine[:, 1:2] * step + turned * jnp.log(mine[:, 2:3])
        upper = (row_at <= lane_at).astype(F32)
        for b in range(2):
            span = slice(b * SPAN, (b + 1) * SPAN)
            row, before_it = id_rows[b + 1], id_rows[b][:, SPAN - 1 :]
            cum = jnp.dot(log_decay[:, span], upper, precision=EXACT, preferred_element_type=F32)
            steps.append(step[:, span])
            cums.append(cum)
            to_end = jnp.where(row == row[:, SPAN - 1 :], jnp.exp(cum[:, SPAN - 1 :] - cum) * step[:, span], 0.0)
            from_start = jnp.where(row == before_it, jnp.exp(cum), 0.0)
            columns[b] = jnp.concatenate([cum, to_end, from_start, jnp.zeros((80, SPAN), F32)], axis=0).T
            wide_row[b] = jnp.dot(columns[b, 120:128], spread[...], precision=EXACT, preferred_element_type=F32)
        d_out[...] = columns[0, 120:128] * columns[1, 120:128]
        d_in[z] = d_out[...]
        for k in range(1, NZ):
            hops["d", k] = send(d_out, d_in.at[z], (s_d_s, s_d_r), k, z_peer[k])

    def expand(b, first):
        return jnp.where(low_lanes, columns[b, :, first : first + 1], columns[b, :, first + 1 : first + 2])

    def conv(j, part_of):
        lanes = slice(part_of * 128, (part_of + 1) * 128)
        start = (WIDE if j == 0 else (j - 1) * COLS) + part_of * 128
        at_channels = pl.ds(pl.multiple_of(c * GROUP + start, 128), 128)
        ext = xbc[j, :, lanes].astype(F32)
        total = conv_b[pl.ds(c * (GROUP // 128) + start // 128, 1), :] + jnp.zeros((ROWS, 128), F32)
        for k in range(3):
            total = total + conv_w[k : k + 1, at_channels] * ext[RIM - 3 + k : RIM - 3 + k + ROWS] * masks[k]
        total = total + conv_w[3:4, at_channels] * ext[RIM:]
        return jax.nn.silu(total).astype(BF16)

    def do_bc(_):
        hops["rim", 0].wait_recv()
        b_matrix = conv(0, 0)
        bc[1] = conv(0, 1)
        bc[0] = b_matrix
        for b in range(2):
            bc[2, b * SPAN : (b + 1) * SPAN] = b_matrix[b * SPAN : (b + 1) * SPAN].T

    def do_st(j):
        hops["rim", j].wait_recv()
        q = j - 1
        for pair in range(2):
            lanes = slice(pair * 128, (pair + 1) * 128)
            heads = conv(j, pair)
            xs[q, :, lanes] = heads
            for b in range(2):
                span = slice(b * SPAN, (b + 1) * SPAN)
                scaled = (heads[span].astype(F32) * expand(b, 16 + 4 * q + 2 * pair)).astype(BF16)
                states[q, b, :, lanes] = jnp.dot(bc[2, span], scaled, preferred_element_type=F32)
        decay = wide_row[1, 7:8, q * COLS : (q + 1) * COLS]
        state_bf[q] = (decay * states[q, 0] + states[q, 1]).astype(BF16).reshape(NZ, 16, COLS)
        st_in[q, z] = state_bf[q, z]
        for k in (4, 3, 5, 2, 6, 1, 7):
            hops["st", q, k] = send(
                state_bf.at[q, turn(z + k, NZ)], st_in.at[q, z], (s_st_s, s_st_r), (q, k), z_peer[k]
            )

    def do_diag(j):
        q = j - 1
        for b in range(2):
            span = slice(b * SPAN, (b + 1) * SPAN)
            scores = lax.dot_general(
                bc[1, span], bc[0, span], (((1,), (1,)), ((), ())), preferred_element_type=F32
            )
            allowed = (id_col[SPAN + b * SPAN : 2 * SPAN + b * SPAN] == id_rows[b + 1]) & (row_at >= lane_at)
            for pair in range(2):
                lanes = slice(pair * 128, (pair + 1) * 128)
                halves = []
                for h in (4 * q + 2 * pair, 4 * q + 2 * pair + 1):
                    gap = jnp.where(allowed, columns[b, :, h : h + 1] - cums[b][h : h + 1], -jnp.inf)
                    halves.append((scores * jnp.exp(gap) * steps[b][h : h + 1]).astype(BF16))
                heads = xs[q, span, lanes]
                zero = jnp.zeros_like(heads)
                both = jnp.concatenate([jnp.where(low_lanes, heads, zero), jnp.where(low_lanes, zero, heads)], axis=0)
                diag = jnp.dot(jnp.concatenate(halves, axis=1), both, preferred_element_type=F32)
                skip = wide_row[2, 3:4, q * COLS + pair * 128 : q * COLS + (pair + 1) * 128]
                osum[q, span, lanes] = diag + skip * heads.astype(F32)

    def do_zs(j):
        q = j - 1
        if ("e", 1) not in hops:
            for k in range(1, NZ):
                hops["d", k].wait_recv()
            per_chip = jnp.concatenate([d_in[k, 7:8] for k in range(NZ)], axis=0)
            wide_z[...] = jnp.dot(per_chip, spread[...], precision=EXACT, preferred_element_type=F32)
            row_decay = per_chip[0:1]
            for k in range(1, NZ):
                row_decay = row_decay * per_chip[k : k + 1]
            e_out[...] = jnp.broadcast_to(row_decay, (8, 128))
            e_in[x] = e_out[...]
            for k in range(1, NX):
                hops["e", k] = send(e_out, e_in.at[x], (s_e_s, s_e_r), k, x_peer[k])
        for k in range(1, NZ):
            hops["st", q, k].wait_recv()
        running = jnp.zeros((16, COLS), F32)
        for k in range(NZ):
            pre[q, k] = running
            running = wide_z[k : k + 1, q * COLS : (q + 1) * COLS] * running + st_in[q, k].astype(F32)
        tot_out[q] = running.astype(BF16)
        tot_in[q, x] = tot_out[q]
        for k in (2, 1, 3):
            hops["t", q, k] = send(tot_out.at[q], tot_in.at[q, x], (s_t_s, s_t_r), (q, k), x_peer[k])

    def do_xs(j):
        q = j - 1
        lanes = slice(q * COLS, (q + 1) * COLS)
        if not entered:
            entered.append(j)
            for k in range(1, NX):
                hops["e", k].wait_recv()
            wide_x[...] = jnp.dot(
                jnp.concatenate([e_in[k] for k in range(NX)], axis=0), spread[...], precision=EXACT,
                preferred_element_type=F32,
            )
        for k in range(1, NX):
            hops["t", q, k].wait_recv()
        entering = jnp.zeros((16, COLS), F32)
        for k in range(NX):
            entering = jnp.where(
                k < x, wide_x[8 * k : 8 * k + 1, lanes] * entering + tot_in[q, k].astype(F32), entering
            )
        for k in range(NZ):
            back_out[q, k] = (pre[q, k] + entering).astype(BF16)
            entering = entering * wide_z[k : k + 1, lanes]
        back_in[q, z] = back_out[q, z]
        for k in (4, 3, 5, 2, 6, 1, 7):
            hops["b", q, k] = send(
                back_out.at[q, turn(z + k, NZ)], back_in.at[q, z], (s_b_s, s_b_r), (q, k), z_peer[k]
            )

    def do_out(j):
        q = j - 1
        first = not left
        left.append(j)
        if first:
            own_gate.wait()
            hops["gate"].wait_recv()
        for k in range(1, NZ):
            hops["b", q, k].wait_recv()
        for pair in range(2):
            lanes = slice(pair * 128, (pair + 1) * 128)
            cols = slice(q * COLS + pair * 128, q * COLS + (pair + 1) * 128)
            carried = back_in[q, :, :, lanes].reshape(STATE, 128)
            later = (wide_row[0, 7:8, cols] * carried.astype(F32) + states[q, 0, :, lanes]).astype(BF16)
            for b, state in ((0, carried), (1, later)):
                span = slice(b * SPAN, (b + 1) * SPAN)
                off = jnp.dot(bc[1, span], state, preferred_element_type=F32) * expand(b, 32 + 4 * q + 2 * pair)
                rows = (osum[q, span, lanes] + off) * jax.nn.silu(gates[b, :, cols].astype(F32))
                gated[q, b, :, lanes] = rows
                squares[b] = rows * rows if first and pair == 0 else squares[b] + rows * rows
        hops["g", q] = send(gated.at[q, 1 - c], gated_sib.at[q], (s_g_s, s_g_r), q, sibling)

    act = {
        "flags": do_flags, "relay": do_relay, "near": do_near, "far": do_far, "toks": do_toks, "mul": do_mul, "steps": do_steps, "pass": do_pass,
        "fin": do_fin, "dt": do_dt, "bc": do_bc, "st": do_st, "diag": do_diag, "zs": do_zs, "xs": do_xs, "out": do_out,
    }
    for word in ORDER:
        if word[0] == "r" and word[1:].isdigit():
            ring_hop(int(word[1]), int(word[2]))
        elif word[-1].isdigit():
            act[word[:-1]](int(word[-1]))
        else:
            act[word](0)

    sums = [jnp.sum(squares[b].T, axis=0, keepdims=True) for b in range(2)]
    sq_out[...] = jnp.concatenate(sums + [jnp.zeros((6, SPAN), F32)], axis=0)
    q_hops = [
        send(sq_out, sq_in.at[k], (s_q_s, s_q_r), k, device) for k, device in enumerate(row_peer)
    ]
    for hop in q_hops:
        hop.wait_recv()
    total = sq_out[...]
    for k in range(7):
        total = total + sq_in[k]
    scale = lax.rsqrt(total / INNER + EPSILON)
    scale = jnp.where(c == 0, scale[0:1], scale[1:2])
    scale = jnp.broadcast_to(scale, (SPAN, SPAN)).T
    for q in range(4):
        hops["g", q].wait_recv()
        for pair in range(2):
            lanes = slice(pair * 128, (pair + 1) * 128)
            for group, rows in ((c, gated[q, c, :, lanes]), (1 - c, gated_sib[q, :, lanes])):
                cols = pl.ds(pl.multiple_of(group * WIDE + q * COLS + pair * 128, 128), 128)
                out[:, cols] = (rows * scale * gain[:, cols]).astype(BF16)
    for copy in started:
        copy.wait_send()


def layer(*arrays):
    sem = pltpu.SemaphoreType.DMA
    vmem, hbm = pl.BlockSpec(memory_space=pltpu.VMEM), pl.BlockSpec(memory_space=pltpu.HBM)

    def pair(*shape):
        return [sem(shape)] * 2 if shape else [sem] * 2

    return pl.pallas_call(
        layer_kernel,
        out_shape=jax.ShapeDtypeStruct((SPAN, 2 * WIDE), BF16),
        in_specs=[hbm] * 13,
        out_specs=vmem,
        scratch_shapes=[
            pltpu.VMEM((2 * HEAD_GROUP, 64), BF16),
            pltpu.VMEM((4, 2 * GROUP), F32),
            pltpu.VMEM((2 * GROUP // 128, 128), F32),
            pltpu.VMEM((1, 2 * HEAD_GROUP), F32),
            pltpu.VMEM((1, 2 * HEAD_GROUP), F32),
            pltpu.VMEM((1, 2 * HEAD_GROUP), F32),
            pltpu.VMEM((1, 2 * HEAD_GROUP), F32),
            pltpu.VMEM((8, 128), F32),
            pltpu.VMEM((1, 2 * WIDE), F32),
            pltpu.VMEM((64, SPAN), jnp.int32),
            pltpu.VMEM((1, SPAN), jnp.int32),
            pltpu.VMEM((NX, ROWS, SLAB), BF16),
            pltpu.VMEM((2, 64, SLAB), BF16),
            pltpu.VMEM((NZ, 2, 80, COLS), BF16),
            pltpu.VMEM((CHUNKS - 1, NZ, 2, 64, COLS), BF16),
            pltpu.VMEM((2, HEAD_GROUP, COLS), BF16),
            pltpu.VMEM((CHUNKS, 3, ROWS, COLS), F32),
            pltpu.VMEM((CHUNKS, 2, 128, COLS), BF16),
            pltpu.VMEM((CHUNKS, 2, 128, COLS), BF16),
            pltpu.VMEM((CHUNKS, 2, ROWS, COLS), BF16),
            pltpu.VMEM((CHUNKS, 2, ROWS, COLS), BF16),
            pltpu.VMEM((3, HEAD_GROUP, ROWS), F32),
            pltpu.VMEM((3, HEAD_GROUP, ROWS), F32),
            pltpu.VMEM((HEAD_GROUP, ROWS), F32),
            pltpu.VMEM((2, 8, SPAN), F32),
            pltpu.VMEM((CHUNKS, RIM + ROWS, COLS), BF16),
            pltpu.VMEM((3 * SPAN, SPAN), F32),
            pltpu.VMEM((3, ROWS, 128), F32),
            pltpu.VMEM((SPAN, WIDE), F32),
            pltpu.VMEM((128, 128), F32),
            pltpu.VMEM((2, SPAN, 128), F32),
            pltpu.VMEM((3, 8, WIDE), F32),
            pltpu.VMEM((3, ROWS, STATE), BF16),
            pltpu.VMEM((4, ROWS, COLS), BF16),
            pltpu.VMEM((4, ROWS, COLS), F32),
            pltpu.VMEM((4, 2, STATE, COLS), F32),
            pltpu.VMEM((4, NZ, 16, COLS), BF16),
            pltpu.VMEM((4, NZ, 16, COLS), BF16),
            pltpu.VMEM((8, 128), F32),
            pltpu.VMEM((NZ, 8, 128), F32),
            pltpu.VMEM((NZ, WIDE), F32),
            pltpu.VMEM((4, NZ, 16, COLS), F32),
            pltpu.VMEM((4, 16, COLS), BF16),
            pltpu.VMEM((4, NX, 16, COLS), BF16),
            pltpu.VMEM((8, 128), F32),
            pltpu.VMEM((NX, 8, 128), F32),
            pltpu.VMEM((8 * NX, WIDE), F32),
            pltpu.VMEM((4, NZ, 16, COLS), BF16),
            pltpu.VMEM((4, NZ, 16, COLS), BF16),
            pltpu.VMEM((2, SPAN, WIDE), BF16),
            pltpu.VMEM((4, 2, SPAN, COLS), F32),
            pltpu.VMEM((4, SPAN, COLS), F32),
            pltpu.VMEM((2, SPAN, 128), F32),
            pltpu.VMEM((8, 128), F32),
            pltpu.VMEM((7, 8, 128), F32),
            sem((10,)),
            sem((CHUNKS,)),
            sem((2,)),
            *pair(CHUNKS + 1),
            *pair(2, 4, CHUNKS),
            *pair(6),
            *pair(5),
            *pair(2, CHUNKS),
            *pair(2, CHUNKS),
            *pair(3),
            *pair(CHUNKS),
            *pair(),
            *pair(),
            *pair(4, NZ),
            *pair(NZ),
            *pair(4, NX),
            *pair(NX),
            *pair(4, NZ),
            *pair(7),
            *pair(4),
        ],
        compiler_params=pltpu.CompilerParams(
            collective_id=0, has_side_effects=True, vmem_limit_bytes=62 * 2**20
        ),
    )(*arrays)


def shards(
    tokens, w_in, w_step, conv_weight, conv_bias, dt_bias, decay_rate, turn_keep, skip, norm_gain, gate,
    segment_ids, turn_start,
):
    return layer(
        tokens, w_in, w_step.T, conv_weight, conv_bias.reshape(-1, 128), dt_bias[None], decay_rate[None],
        turn_keep[None], skip[None], norm_gain[None], gate, segment_ids.reshape(-1, SPAN), turn_start[None],
    )


def solution(mesh):
    in_specs = (
        P("ctx", None),
        P(("ctx", "tr"), "tc"),
        P(("ctx", "tr"), "tc"),
        P(None, "tc"),
        P("tc"),
        P("tc"),
        P("tc"),
        P("tc"),
        P("tc"),
        P("tc"),
        P(("ctx", "tr"), "tc"),
        P(),
        P(("ctx", "tr")),
    )
    out_specs = P(("ctx", "tr"), "tc")
    return jax.shard_map(shards, mesh=mesh, in_specs=in_specs, out_specs=out_specs, check_vma=False)
```

time: 498 us -> 86.6 us (0.17)
  the two profiles are of different devices: /device:TPU:230 before, /device:TPU:1 now
where the time goes in v2:
time: 86.6 us; the launch traced here: 86.5 us
  Pallas kernels  84.6 us (98%)
  local copies, waits for them, and re-layouts  1.88 us (2%)
    pallas_call x1, Pallas kernels, layer(): pl.pallas_call(layer_kernel, out_shape=jax.ShapeDtypeStruct((SPAN, 2 * WI...  84.6 us
    unnamed x1, local copies, waits for them, and re-layouts  1.88 us

profile of v2, /device:TPU:1, one launch (start us, length us, event | category | flops | bytes accessed | tf_op | source)
XLA Modules:
  0.0 86.5 jit_solution(11339909480430899676)
XLA Ops:
  0.0 84.6 %shard_map.127 = bf16[128,2048]{1,0:T(8,128)(2,1)} custom-call(bf16[256,4096]{1,0:T(8,128)(2,1)} %tokens.1, bf16[64,2560]{1,0:T(8,128)(2,1)} %w_in.1, bf16[32,64]{1,0:T(8,128)(2,1)} %bitcast.11, f32[4,2560]{1,0:T(4,128)} %conv_w_hbm.1, f32[20,128]{1,0:T(8,128)} %bitcast.10, f32[1,32]{1,0:T(1,128)} %bitcast.13, f32[1,32]{1,0:T(1,128)} %bitcast.14, ...), custom_call_target="tpu_custom_call" | custom-call | tf_op jit(solution)/shard_map/pallas_call | solution.py:480
  84.6 1.9 %copy.15 = bf16[128,2048]{1,0:T(8,128)(2,1)} copy(bf16[128,2048]{1,0:T(8,128)(2,1)} %shard_map.127) | data formatting | bytes 1048576

commit v3 on v2

--- a/solution.py
+++ b/solution.py
@@ -40,18 +40,18 @@
     )
 
 
-def meet(devices):
+def greet(devices):
     barrier = pltpu.get_barrier_semaphore()
     for device in devices:
         pl.semaphore_signal(barrier, inc=1, device_id=device, device_id_type=MESH)
-    pl.semaphore_wait(barrier, len(devices))
+    return len(devices)
 
 
 ORDER = (
     "r02", "r01", "r00", "relay", "r12", "r11", "r10", "r22", "r20", "near", "r32", "r03", "far", "r30",
     "r21", "toks", "mul2", "r04", "mul0", "r31", "pass2", "r13", "r14", "mul1", "flags", "pass0", "r23",
     "r24", "pass1", "r33", "steps", "r34", "fin0", "fin2", "mul3", "mul4", "dt", "bc", "pass3", "fin1", "st2",
-    "pass4", "fin3", "st1", "diag2", "diag1", "st3", "zs2", "fin4", "zs1", "st4", "xs2", "xs1", "zs3", "zs4",
+    "pass4", "drain", "fin3", "st1", "diag2", "diag1", "st3", "zs2", "fin4", "zs1", "st4", "xs2", "xs1", "zs3", "drain", "zs4",
     "xs3", "diag3", "xs4", "diag4", "out1", "out3", "out2", "out4",
 )
 
@@ -79,6 +79,9 @@
     sibling = {"tr": 1 - c}
     after, before = {"ctx": turn(ctx + 1, NX * NZ)}, {"ctx": turn(ctx + NX * NZ - 1, NX * NZ)}
 
+    z_cross = [{**z_right, "tr": 1 - c}, {**z_left, "tr": 1 - c}]
+    greeted = greet(z_peer[1:] + x_peer[1:] + row_peer + [after, before] + z_cross)
+
     def columns_of(group, j):
         start = WIDE if j == 0 else (j - 1) * COLS
         return pl.ds(pl.multiple_of(group * GROUP + start, 128), COLS)
@@ -126,7 +129,7 @@
     wg0[z, c, 64:80, :] = step_rows[c]
     flags[c] = jnp.broadcast_to(turns[...].astype(F32), (8, SPAN))
 
-    meet(z_peer[1:] + x_peer[1:] + row_peer + [after, before])
+    pl.semaphore_wait(pltpu.get_barrier_semaphore(), greeted)
 
     started = []
 
@@ -136,6 +139,13 @@
         else:
             copy = remote(src, dst, sems[0].at[index], sems[1].at[index], device)
         copy.start()
+        started.append(copy)
+        return copy
+
+    def send_all(pieces, whole, sems):
+        for src, dst, device in pieces:
+            remote(src, dst, sems[0], sems[1], device).start()
+        copy = remote(whole[0], whole[1], sems[0], sems[1], pieces[0][2])
         started.append(copy)
         return copy
 
@@ -163,17 +173,32 @@
     hops = {}
 
     def ring_hop(h, j):
+        sems = (s_ring_s, s_ring_r)
         if h == 0:
             local[j].wait()
-            for copy in from_sibling[j]:
-                copy.wait_recv()
         for way, sign, device in ((0, -1, z_right), (1, 1, z_left)):
-            if h > 0:
-                hops["r", way, h - 1, j].wait_recv()
+            if h == 0:
+                other = z_cross[way]
+                target = wg0.at[z, c, pl.ds(0, 64)] if j == 0 else wg.at[j - 1, z, c]
+                hops["r", way, 0, j] = send(block(j, z, c), block(j, z, c), sems, (way, 0, j), device)
+                hops["rx", way, j] = [send(w_in.at[:, columns_of(1 - c, j)], target, sems, (way, 4, j), other)]
+                if j == 0:
+                    hops["rx", way, j].append(
+                        send(step_rows.at[1 - c], wg0.at[z, c, pl.ds(64, 16)], sems, (way, 5, j), other)
+                    )
+                continue
+            hops["r", way, h - 1, j].wait_recv()
+            if h == 1:
+                for copy in hops["rx", way, j]:
+                    copy.wait_recv()
             slot = turn(z + sign * h + NZ, NZ)
             piece = None if h < 3 else way
             ref = block(j, slot, piece)
-            hops["r", way, h, j] = send(ref, ref, (s_ring_s, s_ring_r), (way, h, j), device)
+            hops["r", way, h, j] = send(ref, ref, sems, (way, h, j), device)
+
+    def drain(keep):
+        while len(started) > keep:
+            started.pop(0).wait_send()
 
     row_at = lax.broadcasted_iota(jnp.int32, (SPAN, SPAN), 0)
     lane_at = lax.broadcasted_iota(jnp.int32, (SPAN, SPAN), 1)
@@ -232,6 +257,8 @@
     def do_mul(j):
         for way in range(2):
             hops["r", way, 3, j].wait_recv()
+        for copy in from_sibling[j]:
+            copy.wait_recv()
         w = (wg0[:, :, :64, :] if j == 0 else wg[j - 1]).reshape(SLAB, COLS)
         far = jnp.dot(toks[2], w, preferred_element_type=F32)
         rel_out[j, 0] = far[:128].astype(BF16)
@@ -295,8 +322,8 @@
             wide_row[b] = jnp.dot(columns[b, 120:128], spread[...], precision=EXACT, preferred_element_type=F32)
         d_out[...] = columns[0, 120:128] * columns[1, 120:128]
         d_in[z] = d_out[...]
-        for k in range(1, NZ):
-            hops["d", k] = send(d_out, d_in.at[z], (s_d_s, s_d_r), k, z_peer[k])
+        seven = d_in.at[pl.ds(0, 7)]
+        hops["d"] = send_all([(d_out, d_in.at[z], z_peer[k]) for k in range(1, NZ)], (seven, seven), (s_d_s, s_d_r))
 
     def expand(b, first):
         return jnp.where(low_lanes, columns[b, :, first : first + 1], columns[b, :, first + 1 : first + 2])
@@ -334,10 +361,11 @@
         decay = wide_row[1, 7:8, q * COLS : (q + 1) * COLS]
         state_bf[q] = (decay * states[q, 0] + states[q, 1]).astype(BF16).reshape(NZ, 16, COLS)
         st_in[q, z] = state_bf[q, z]
-        for k in (4, 3, 5, 2, 6, 1, 7):
-            hops["st", q, k] = send(
-                state_bf.at[q, turn(z + k, NZ)], st_in.at[q, z], (s_st_s, s_st_r), (q, k), z_peer[k]
-            )
+        hops["st", q] = send_all(
+            [(state_bf.at[q, turn(z + k, NZ)], st_in.at[q, z], z_peer[k]) for k in (4, 3, 5, 2, 6, 1, 7)],
+            (state_bf.at[q, pl.ds(0, 7)], st_in.at[q, pl.ds(0, 7)]),
+            (s_st_s.at[q], s_st_r.at[q]),
+        )
 
     def do_diag(j):
         q = j - 1
@@ -362,9 +390,8 @@
 
     def do_zs(j):
         q = j - 1
-        if ("e", 1) not in hops:
-            for k in range(1, NZ):
-                hops["d", k].wait_recv()
+        if "e" not in hops:
+            hops["d"].wait_recv()
             per_chip = jnp.concatenate([d_in[k, 7:8] for k in range(NZ)], axis=0)
             wide_z[...] = jnp.dot(per_chip, spread[...], precision=EXACT, preferred_element_type=F32)
             row_decay = per_chip[0:1]
@@ -372,32 +399,31 @@
                 row_decay = row_decay * per_chip[k : k + 1]
             e_out[...] = jnp.broadcast_to(row_decay, (8, 128))
             e_in[x] = e_out[...]
-            for k in range(1, NX):
-                hops["e", k] = send(e_out, e_in.at[x], (s_e_s, s_e_r), k, x_peer[k])
-        for k in range(1, NZ):
-            hops["st", q, k].wait_recv()
+            three = e_in.at[pl.ds(0, 3)]
+            hops["e"] = send_all([(e_out, e_in.at[x], x_peer[k]) for k in (2, 1, 3)], (three, three), (s_e_s, s_e_r))
+        hops["st", q].wait_recv()
         running = jnp.zeros((16, COLS), F32)
         for k in range(NZ):
             pre[q, k] = running
             running = wide_z[k : k + 1, q * COLS : (q + 1) * COLS] * running + st_in[q, k].astype(F32)
         tot_out[q] = running.astype(BF16)
         tot_in[q, x] = tot_out[q]
-        for k in (2, 1, 3):
-            hops["t", q, k] = send(tot_out.at[q], tot_in.at[q, x], (s_t_s, s_t_r), (q, k), x_peer[k])
+        three = tot_in.at[q, pl.ds(0, 3)]
+        hops["t", q] = send_all(
+            [(tot_out.at[q], tot_in.at[q, x], x_peer[k]) for k in (2, 1, 3)], (three, three), (s_t_s.at[q], s_t_r.at[q])
+        )
 
     def do_xs(j):
         q = j - 1
         lanes = slice(q * COLS, (q + 1) * COLS)
         if not entered:
             entered.append(j)
-            for k in range(1, NX):
-                hops["e", k].wait_recv()
+            hops["e"].wait_recv()
             wide_x[...] = jnp.dot(
                 jnp.concatenate([e_in[k] for k in range(NX)], axis=0), spread[...], precision=EXACT,
                 preferred_element_type=F32,
             )
-        for k in range(1, NX):
-            hops["t", q, k].wait_recv()
+        hops["t", q].wait_recv()
         entering = jnp.zeros((16, COLS), F32)
         for k in range(NX):
             entering = jnp.where(
@@ -407,10 +433,11 @@
             back_out[q, k] = (pre[q, k] + entering).astype(BF16)
             entering = entering * wide_z[k : k + 1, lanes]
         back_in[q, z] = back_out[q, z]
-        for k in (4, 3, 5, 2, 6, 1, 7):
-            hops["b", q, k] = send(
-                back_out.at[q, turn(z + k, NZ)], back_in.at[q, z], (s_b_s, s_b_r), (q, k), z_peer[k]
-            )
+        hops["b", q] = send_all(
+            [(back_out.at[q, turn(z + k, NZ)], back_in.at[q, z], z_peer[k]) for k in (4, 3, 5, 2, 6, 1, 7)],
+            (back_out.at[q, pl.ds(0, 7)], back_in.at[q, pl.ds(0, 7)]),
+            (s_b_s.at[q], s_b_r.at[q]),
+        )
 
     def do_out(j):
         q = j - 1
@@ -419,8 +446,7 @@
         if first:
             own_gate.wait()
             hops["gate"].wait_recv()
-        for k in range(1, NZ):
-            hops["b", q, k].wait_recv()
+        hops["b", q].wait_recv()
         for pair in range(2):
             lanes = slice(pair * 128, (pair + 1) * 128)
             cols = slice(q * COLS + pair * 128, q * COLS + (pair + 1) * 128)
@@ -436,7 +462,7 @@
 
     act = {
         "flags": do_flags, "relay": do_relay, "near": do_near, "far": do_far, "toks": do_toks, "mul": do_mul, "steps": do_steps, "pass": do_pass,
-        "fin": do_fin, "dt": do_dt, "bc": do_bc, "st": do_st, "diag": do_diag, "zs": do_zs, "xs": do_xs, "out": do_out,
+        "fin": do_fin, "dt": do_dt, "bc": do_bc, "st": do_st, "diag": do_diag, "drain": lambda _: drain(14), "zs": do_zs, "xs": do_xs, "out": do_out,
     }
     for word in ORDER:
         if word[0] == "r" and word[1:].isdigit():
@@ -448,11 +474,9 @@
 
     sums = [jnp.sum(squares[b].T, axis=0, keepdims=True) for b in range(2)]
     sq_out[...] = jnp.concatenate(sums + [jnp.zeros((6, SPAN), F32)], axis=0)
-    q_hops = [
-        send(sq_out, sq_in.at[k], (s_q_s, s_q_r), k, device) for k, device in enumerate(row_peer)
-    ]
-    for hop in q_hops:
-        hop.wait_recv()
+    send_all(
+        [(sq_out, sq_in.at[k], device) for k, device in enumerate(row_peer)], (sq_in, sq_in), (s_q_s, s_q_r)
+    ).wait_recv()
     total = sq_out[...]
     for k in range(7):
         total = total + sq_in[k]
@@ -466,8 +490,7 @@
             for group, rows in ((c, gated[q, c, :, lanes]), (1 - c, gated_sib[q, :, lanes])):
                 cols = pl.ds(pl.multiple_of(group * WIDE + q * COLS + pair * 128, 128), 128)
                 out[:, cols] = (rows * scale * gain[:, cols]).astype(BF16)
-    for copy in started:
-        copy.wait_send()
+    drain(0)
 
 
 def layer(*arrays):
@@ -542,7 +565,7 @@
             sem((CHUNKS,)),
             sem((2,)),
             *pair(CHUNKS + 1),
-            *pair(2, 4, CHUNKS),
+            *pair(2, 6, CHUNKS),
             *pair(6),
             *pair(5),
             *pair(2, CHUNKS),
@@ -551,12 +574,12 @@
             *pair(CHUNKS),
             *pair(),
             *pair(),
-            *pair(4, NZ),
-            *pair(NZ),
-            *pair(4, NX),
-            *pair(NX),
-            *pair(4, NZ),
-            *pair(7),
+            *pair(4),
+            *pair(),
+            *pair(4),
+            *pair(),
+            *pair(4),
+            *pair(),
             *pair(4),
         ],
         compiler_params=pltpu.CompilerParams(

time: 86.6 us -> 84.9 us (0.980)
  Pallas kernels: 84.6 us -> 82.8 us
    pallas_call x1, Pallas kernels: 84.6 us -> 82.8 us  [layer(): pl.pallas_call(layer_kernel, out_shape=jax.ShapeDtypeStruct((SPAN, 2 * WI...]
where the time goes in v3:
time: 84.9 us; the launch traced here: 84.7 us
  Pallas kernels  82.8 us (98%)
  local copies, waits for them, and re-layouts  1.88 us (2%)
    pallas_call x1, Pallas kernels, layer(): pl.pallas_call(layer_kernel, out_shape=jax.ShapeDtypeStruct((SPAN, 2 * WI...  82.8 us
    unnamed x1, local copies, waits for them, and re-layouts  1.88 us

profile of v3, /device:TPU:1, one launch (start us, length us, event | category | flops | bytes accessed | tf_op | source)
XLA Modules:
  0.0 84.7 jit_solution(14676411479075409731)
XLA Ops:
  0.0 82.8 %shard_map.127 = bf16[128,2048]{1,0:T(8,128)(2,1)} custom-call(bf16[256,4096]{1,0:T(8,128)(2,1)} %tokens.1, bf16[64,2560]{1,0:T(8,128)(2,1)} %w_in.1, bf16[32,64]{1,0:T(8,128)(2,1)} %bitcast.11, f32[4,2560]{1,0:T(4,128)} %conv_w_hbm.1, f32[20,128]{1,0:T(8,128)} %bitcast.10, f32[1,32]{1,0:T(1,128)} %bitcast.13, f32[1,32]{1,0:T(1,128)} %bitcast.14, ...), custom_call_target="tpu_custom_call" | custom-call | tf_op jit(solution)/shard_map/pallas_call | solution.py:503
  82.9 1.9 %copy.15 = bf16[128,2048]{1,0:T(8,128)(2,1)} copy(bf16[128,2048]{1,0:T(8,128)(2,1)} %shard_map.127) | data formatting | bytes 1048576

commit v4 on v3

--- a/solution.py
+++ b/solution.py
@@ -19,6 +19,7 @@
 WIDE = 1024
 COLS = 256
 CHUNKS = 5
+LAST = 4
 RIM = 16
 MESH = pl.DeviceIdType.MESH
 F32, BF16 = jnp.float32, jnp.bfloat16
@@ -48,17 +49,17 @@
 
 
 ORDER = (
-    "r02", "r01", "r00", "relay", "r12", "r11", "r10", "r22", "r20", "near", "r32", "r03", "far", "r30",
-    "r21", "toks", "mul2", "r04", "mul0", "r31", "pass2", "r13", "r14", "mul1", "flags", "pass0", "r23",
-    "r24", "pass1", "r33", "steps", "r34", "fin0", "fin2", "mul3", "mul4", "dt", "bc", "pass3", "fin1", "st2",
-    "pass4", "drain", "fin3", "st1", "diag2", "diag1", "st3", "zs2", "fin4", "zs1", "st4", "xs2", "xs1", "zs3", "drain", "zs4",
-    "xs3", "diag3", "xs4", "diag4", "out1", "out3", "out2", "out4",
+    "r02", "r00", "r01", "flags", "r12", "r10", "relay", "r11", "r22", "r20", "near", "r21", "r30", "far",
+    "r32", "r03", "toks", "r31", "mul0", "r04", "mul2", "steps", "r13", "mul1", "pass0", "r14", "r23",
+    "pass2", "r24", "r33", "pass1", "dt", "fin0", "r34", "mul3", "fin2", "mul4", "bc", "pass3", "fin1",
+    "pass4", "drain", "st2", "st1", "fin3", "edge", "zs2", "zs1", "fin4", "st3", "st4", "xs1", "xs2", "zs3",
+    "drain", "zs4", "diag2", "diag1", "xs3", "out1", "diag4", "xs4", "out2", "diag3", "out3", "out4",
 )
 
 
 def layer_kernel(
-    tokens, w_in, w_step_hbm, conv_w_hbm, conv_b_hbm, dt_bias_hbm, rate_hbm, keep_hbm, skip_hbm, gain_hbm, gate, ids_hbm,
-    turns_hbm, out, w_step, conv_w, conv_b, dt_bias, rate, keep, skip_row, par, gain, ids, turns,
+    tokens, w_in, w_step_hbm, conv_w_hbm, conv_b_hbm, dt_bias_hbm, rate_hbm, keep_hbm, skip_hbm, gate, ids_hbm,
+    turns_hbm, out, w_step, conv_w, conv_b, dt_bias, rate, keep, skip_row, par, ids, turns,
     toks, tok_relay, wg0, wg, step_rows, part, rel_out, rel_in, nb_out, nb_in, dt_out, dt_in, dt_own, flags,
     xbc, id_col, masks, spread, head_col, columns, wide_row, bc, xs, osum, states, state_bf, st_in, d_out, d_in,
     wide_z, pre, tot_out, tot_in, e_out, e_in, wide_x, back_out, back_in, gates, gated, gated_sib, squares, sq_out, sq_in,
@@ -100,7 +101,7 @@
     for k, (src, dst) in enumerate(
         (
             (w_step_hbm, w_step), (turns_hbm, turns), (ids_hbm, ids), (conv_w_hbm, conv_w), (conv_b_hbm, conv_b),
-            (dt_bias_hbm, dt_bias), (rate_hbm, rate), (keep_hbm, keep), (skip_hbm, skip_row), (gain_hbm, gain),
+            (dt_bias_hbm, dt_bias), (rate_hbm, rate), (keep_hbm, keep), (skip_hbm, skip_row),
         )
     ):
         small.append(pltpu.make_async_copy(src, dst, s_small.at[k]))
@@ -281,23 +282,60 @@
                 dt_out[d - 1] = sums
                 hops["dt", d] = send(dt_out.at[d - 1], dt_in.at[d - 1], (s_dt_s, s_dt_r), d - 1, x_peer[d])
 
+    body = ROWS - RIM
+
+    def send_sums(j, way, device):
+        sems = (s_nb_s, s_nb_r)
+        if j < LAST:
+            hops["nb", way, j] = send(nb_out.at[j, way], nb_in.at[j, way], sems, (way, j), device)
+            return
+        rows = pl.ds(0, body)
+        hops["nb", way, j] = send(nb_out.at[j, way, rows], nb_in.at[j, way, rows], sems, (way, j), device)
+
+    def send_edge(way, device):
+        rows = pl.ds(body, RIM)
+        hops["edge", way] = send(
+            nb_out.at[LAST, way, rows], nb_in.at[LAST, way, rows], (s_nb_s, s_nb_r), (way, CHUNKS), device
+        )
+
     def do_pass(j):
+        nb_out[j, 0, 128:] = part[j, 1, 128:].astype(BF16)
+        nb_out[j, 1, :128] = part[j, 2, :128].astype(BF16)
+        if j == LAST:
+            send_edge(0, x_right)
         hops["rel", 0, j].wait_recv()
         nb_out[j, 0, :128] = (part[j, 1, :128] + rel_in[j, 0].astype(F32)).astype(BF16)
-        nb_out[j, 0, 128:] = part[j, 1, 128:].astype(BF16)
-        hops["nb", 0, j] = send(nb_out.at[j, 0], nb_in.at[j, 0], (s_nb_s, s_nb_r), (0, j), x_right)
+        if j < LAST:
+            send_sums(j, 0, x_right)
         hops["rel", 1, j].wait_recv()
-        nb_out[j, 1, :128] = part[j, 2, :128].astype(BF16)
         nb_out[j, 1, 128:] = (part[j, 2, 128:] + rel_in[j, 1].astype(F32)).astype(BF16)
-        hops["nb", 1, j] = send(nb_out.at[j, 1], nb_in.at[j, 1], (s_nb_s, s_nb_r), (1, j), x_left)
+        if j == LAST:
+            send_edge(1, x_left)
+            send_sums(j, 0, x_right)
+        send_sums(j, 1, x_left)
+
+    def add_up(j, rows):
+        return (part[j, 0, rows] + (nb_in[j, 0, rows].astype(F32) + nb_in[j, 1, rows].astype(F32))).astype(BF16)
+
+    def send_rim(j):
+        hops["rim", j] = send(
+            xbc.at[j, pl.ds(ROWS, RIM)], xbc.at[j, pl.ds(0, RIM)], (s_rim_s, s_rim_r), j, after
+        )
+
+    def do_edge(_):
+        hops["edge", 0].wait_recv()
+        hops["edge", 1].wait_recv()
+        xbc[LAST, ROWS:] = add_up(LAST, slice(body, ROWS))
+        send_rim(LAST)
 
     def do_fin(j):
         hops["nb", 0, j].wait_recv()
         hops["nb", 1, j].wait_recv()
-        xbc[j, RIM:] = (part[j, 0] + (nb_in[j, 0].astype(F32) + nb_in[j, 1].astype(F32))).astype(BF16)
-        hops["rim", j] = send(
-            xbc.at[j, pl.ds(ROWS, RIM)], xbc.at[j, pl.ds(0, RIM)], (s_rim_s, s_rim_r), j, after
-        )
+        if j == LAST:
+            xbc[j, RIM:ROWS] = add_up(j, slice(0, body))
+        else:
+            xbc[j, RIM:] = add_up(j, slice(0, ROWS))
+            send_rim(j)
 
     cums, steps, entered, left = [], [], [], []
 
@@ -462,7 +500,7 @@
 
     act = {
         "flags": do_flags, "relay": do_relay, "near": do_near, "far": do_far, "toks": do_toks, "mul": do_mul, "steps": do_steps, "pass": do_pass,
-        "fin": do_fin, "dt": do_dt, "bc": do_bc, "st": do_st, "diag": do_diag, "drain": lambda _: drain(14), "zs": do_zs, "xs": do_xs, "out": do_out,
+        "fin": do_fin, "edge": do_edge, "dt": do_dt, "bc": do_bc, "st": do_st, "diag": do_diag, "drain": lambda _: drain(14), "zs": do_zs, "xs": do_xs, "out": do_out,
     }
     for word in ORDER:
         if word[0] == "r" and word[1:].isdigit():
@@ -489,7 +527,7 @@
             lanes = slice(pair * 128, (pair + 1) * 128)
             for group, rows in ((c, gated[q, c, :, lanes]), (1 - c, gated_sib[q, :, lanes])):
                 cols = pl.ds(pl.multiple_of(group * WIDE + q * COLS + pair * 128, 128), 128)
-                out[:, cols] = (rows * scale * gain[:, cols]).astype(BF16)
+                out[:, cols] = rows * scale
     drain(0)
 
 
@@ -502,8 +540,8 @@
 
     return pl.pallas_call(
         layer_kernel,
-        out_shape=jax.ShapeDtypeStruct((SPAN, 2 * WIDE), BF16),
-        in_specs=[hbm] * 13,
+        out_shape=jax.ShapeDtypeStruct((SPAN, 2 * WIDE), F32),
+        in_specs=[hbm] * 12,
         out_specs=vmem,
         scratch_shapes=[
             pltpu.VMEM((2 * HEAD_GROUP, 64), BF16),
@@ -514,7 +552,6 @@
             pltpu.VMEM((1, 2 * HEAD_GROUP), F32),
             pltpu.VMEM((1, 2 * HEAD_GROUP), F32),
             pltpu.VMEM((8, 128), F32),
-            pltpu.VMEM((1, 2 * WIDE), F32),
             pltpu.VMEM((64, SPAN), jnp.int32),
             pltpu.VMEM((1, SPAN), jnp.int32),
             pltpu.VMEM((NX, ROWS, SLAB), BF16),
@@ -561,7 +598,7 @@
             pltpu.VMEM((2, SPAN, 128), F32),
             pltpu.VMEM((8, 128), F32),
             pltpu.VMEM((7, 8, 128), F32),
-            sem((10,)),
+            sem((9,)),
             sem((CHUNKS,)),
             sem((2,)),
             *pair(CHUNKS + 1),
@@ -569,7 +606,7 @@
             *pair(6),
             *pair(5),
             *pair(2, CHUNKS),
-            *pair(2, CHUNKS),
+            *pair(2, CHUNKS + 1),
             *pair(3),
             *pair(CHUNKS),
             *pair(),
@@ -592,10 +629,11 @@
     tokens, w_in, w_step, conv_weight, conv_bias, dt_bias, decay_rate, turn_keep, skip, norm_gain, gate,
     segment_ids, turn_start,
 ):
-    return layer(
+    rows = layer(
         tokens, w_in, w_step.T, conv_weight, conv_bias.reshape(-1, 128), dt_bias[None], decay_rate[None],
-        turn_keep[None], skip[None], norm_gain[None], gate, segment_ids.reshape(-1, SPAN), turn_start[None],
+        turn_keep[None], skip[None], gate, segment_ids.reshape(-1, SPAN), turn_start[None],
     )
+    return (rows * norm_gain[None, :]).astype(BF16)
 
 
 def solution(mesh):

time: 84.9 us -> 80.8 us (0.952)
  Pallas kernels: 82.8 us -> 78.6 us
  other arithmetic: 0 us -> 2.1 us
  local copies, waits for them, and re-layouts: 1.88 us -> 0.01 us
    pallas_call x1, Pallas kernels: 82.8 us -> 78.6 us  [layer(): pl.pallas_call(layer_kernel, out_shape=jax.ShapeDtypeStruct((SPAN, 2 * WI...]
    convert_element_type x0 -> x1, other arithmetic: none -> 2.1 us  [shards(): return (rows * norm_gain[None, :]).astype(BF16)]
    unnamed x1 -> x2, local copies, waits for them, and re-layouts: 1.88 us -> 0.01 us
where the time goes in v4:
time: 80.8 us; the launch traced here: 80.7 us
  Pallas kernels  78.6 us (97%)
  other arithmetic  2.1 us (3%)
    pallas_call x1, Pallas kernels, layer(): pl.pallas_call(layer_kernel, out_shape=jax.ShapeDtypeStruct((SPAN, 2 * WI...  78.6 us
    convert_element_type x1, other arithmetic, shards(): return (rows * norm_gain[None, :]).astype(BF16)  2.1 us

profile of v4, /device:TPU:1, one launch (start us, length us, event | category | flops | bytes accessed | tf_op | source)
XLA Modules:
  0.0 80.7 jit_solution(3191268768732720820)
XLA Ops:
  0.0 0.0 copy-start
  0.0 78.6 %shard_map.127 = f32[128,2048]{1,0:T(8,128)} custom-call(bf16[256,4096]{1,0:T(8,128)(2,1)} %tokens.1, bf16[64,2560]{1,0:T(8,128)(2,1)} %w_in.1, bf16[32,64]{1,0:T(8,128)(2,1)} %bitcast.10, f32[4,2560]{1,0:T(4,128)} %conv_w_hbm.1, f32[20,128]{1,0:T(8,128)} %bitcast.9, f32[1,32]{1,0:T(1,128)} %bitcast.11, f32[1,32]{1,0:T(1,128)} %bitcast.12, ...), custom_call_target="tpu_custom_call" | custom-call | tf_op jit(solution)/shard_map/pallas_call | solution.py:541
  78.6 0.0 copy-done
  78.6 2.1 %multiply_convert_fusion = bf16[128,2048]{1,0:T(8,128)(2,1)} fusion(f32[128,2048]{1,0:T(8,128)} %shard_map.127, f32[2048]{0:T(1024)S(1)} %copy-done), kind=kLoop, calls=%fused_computation | loop fusion | flops 524288 | bytes 1581056 | tf_op jit(solution)/shard_map/convert_element_type | solution.py:636
Async XLA Ops:
  0.0 78.6 %copy-start = (f32[2048]{0:T(1024)S(1)}, f32[2048]{0:T(1024)}, u32[]{:S(2)}) copy-start(f32[2048]{0:T(1024)} %param.22) | copy-start | bytes 24580

commit v5 on v4

--- a/solution.py
+++ b/solution.py
@@ -52,7 +52,7 @@
     "r02", "r00", "r01", "flags", "r12", "r10", "relay", "r11", "r22", "r20", "near", "r21", "r30", "far",
     "r32", "r03", "toks", "r31", "mul0", "r04", "mul2", "steps", "r13", "mul1", "pass0", "r14", "r23",
     "pass2", "r24", "r33", "pass1", "dt", "fin0", "r34", "mul3", "fin2", "mul4", "bc", "pass3", "fin1",
-    "pass4", "drain", "st2", "st1", "fin3", "edge", "zs2", "zs1", "fin4", "st3", "st4", "xs1", "xs2", "zs3",
+    "pass4", "drain", "st2", "st1", "fin3", "edge", "zs2", "zs1", "st3", "fin4", "st4", "xs1", "xs2", "zs3",
     "drain", "zs4", "diag2", "diag1", "xs3", "out1", "diag4", "xs4", "out2", "diag3", "out3", "out4",
 )
 

time: 80.8 us -> 80.9 us (level)
  no operation moved by 1% of the time
where the time goes in v5:
time: 80.9 us; the launch traced here: 80.8 us
  Pallas kernels  78.6 us (97%)
  other arithmetic  2.1 us (3%)
    pallas_call x1, Pallas kernels, layer(): pl.pallas_call(layer_kernel, out_shape=jax.ShapeDtypeStruct((SPAN, 2 * WI...  78.6 us
    convert_element_type x1, other arithmetic, shards(): return (rows * norm_gain[None, :]).astype(BF16)  2.1 us

profile of v5, /device:TPU:1, one launch (start us, length us, event | category | flops | bytes accessed | tf_op | source)
XLA Modules:
  0.0 80.8 jit_solution(12842082603680315912)
XLA Ops:
  0.0 0.0 copy-start
  0.0 78.6 %shard_map.127 = f32[128,2048]{1,0:T(8,128)} custom-call(bf16[256,4096]{1,0:T(8,128)(2,1)} %tokens.1, bf16[64,2560]{1,0:T(8,128)(2,1)} %w_in.1, bf16[32,64]{1,0:T(8,128)(2,1)} %bitcast.10, f32[4,2560]{1,0:T(4,128)} %conv_w_hbm.1, f32[20,128]{1,0:T(8,128)} %bitcast.9, f32[1,32]{1,0:T(1,128)} %bitcast.11, f32[1,32]{1,0:T(1,128)} %bitcast.12, ...), custom_call_target="tpu_custom_call" | custom-call | tf_op jit(solution)/shard_map/pallas_call | solution.py:541
  78.6 0.0 copy-done
  78.7 2.1 %multiply_convert_fusion = bf16[128,2048]{1,0:T(8,128)(2,1)} fusion(f32[128,2048]{1,0:T(8,128)} %shard_map.127, f32[2048]{0:T(1024)S(1)} %copy-done), kind=kLoop, calls=%fused_computation | loop fusion | flops 524288 | bytes 1581056 | tf_op jit(solution)/shard_map/convert_element_type | solution.py:636
Async XLA Ops:
  0.0 78.6 %copy-start = (f32[2048]{0:T(1024)S(1)}, f32[2048]{0:T(1024)}, u32[]{:S(2)}) copy-start(f32[2048]{0:T(1024)} %param.22) | copy-start | bytes 24580
